TPU v7x, 512 devices: a whole 4x4x16 slice. The times are simulated.
512 devices in a mesh: row: 16 (over y_lo, x, core), col: 32 (over z, y_hi).
Axes of the slice: x: 4, y: 4 (y_hi: 2, y_lo: 2; y = y_hi * 2 + y_lo), z: 16, core: 2. Of those that a mesh axis runs over, the one named last changes fastest.
Arguments:
- projected: bfloat16 [3, 2048, 16, 32, 128], P(None, None, 'row', 'col'), may hold values from -6 to 6
- short_taps: float32 [3, 2048, 3], replicated, may hold values from -3 to 3
- long_filter: bfloat16 [2048, 16, 32, 128], P(None, 'row', 'col'), may hold values from -6 to 6
- skip_gain: float32 [2048], replicated, may hold values from 0.5 to 1.5
- cotangent: bfloat16 [2048, 16, 32, 128], P(None, 'row', 'col'), may hold values from -6 to 6
Outputs:
- filter_grad: bfloat16 [2048, 16, 32, 128], P(None, 'row', 'col')
- projected_grad: bfloat16 [3, 2048, 16, 32, 128], P(None, None, 'row', 'col')
All inputs are finite; a program needn't handle non-finite values.
Results may differ from a plain program's by a relative error of at most 0.0049.
Values may be sent and summed in bfloat16 or wider, within the bound.
A program may use at most 64 MiB of HBM per device.

v0:
```python
import math

import jax
import jax.numpy as jnp
from jax import lax
from jax.sharding import PartitionSpec as P


def from_behind(array, axis, by):
    devices = lax.axis_size(axis)
    return lax.ppermute(array, axis, [(i, (i + by) % devices) for i in range(devices)])


def contract(form, left, right):
    return jnp.einsum(form, left, right, precision=lax.Precision.HIGHEST)


def dft_table(length, direction):
    indices = jnp.arange(length, dtype=jnp.int32)
    product_mod = indices[:, None] * indices[None, :] % length
    angles = product_mod.astype(jnp.float32) * (2.0 * math.pi / length)
    return (jnp.cos(angles), direction * jnp.sin(angles))


def block_table(length, direction):
    cosine, sine = dft_table(length, direction)
    return jnp.stack([jnp.stack([cosine, sine]), jnp.stack([-sine, cosine])])


def rotation(numerators, modulus, direction):
    angles = numerators.astype(jnp.float32) * (2.0 * math.pi / modulus)
    return (jnp.cos(angles), direction * jnp.sin(angles))


def rotate_pair(values, factor_real, factor_imag):
    return jnp.stack(
        [
            values[0] * factor_real - values[1] * factor_imag,
            values[0] * factor_imag + values[1] * factor_real,
        ]
    )


def times_pair(left, right, conjugate):
    right_imag = -right[1] if conjugate else right[1]
    return jnp.stack(
        [left[0] * right[0] - left[1] * right_imag, left[0] * right_imag + left[1] * right[0]]
    )


def spread_steps(row_count, column_count, turn_count):
    slots = (
        jnp.arange(row_count, dtype=jnp.int32)[:, None, None] * column_count
        + jnp.arange(column_count, dtype=jnp.int32)[None, :, None]
    )
    return (
        slots
        * jnp.arange(turn_count, dtype=jnp.int32)[None, None, :]
        % (turn_count * row_count * column_count)
    )


def cross_steps(row_count, column_count):
    return (
        jnp.arange(row_count, dtype=jnp.int32)[:, None, None]
        * jnp.arange(column_count, dtype=jnp.int32)[None, :, None]
        % (row_count * column_count)
    )


def forward_spectrum(lines, row_count, column_count):
    turn_count = lines.shape[-1]
    devices_all = row_count * column_count
    sequence_length = turn_count * devices_all
    cosine_turns, sine_turns = dft_table(turn_count, -1.0)
    section = contract("fabs,wsk->wfabk", lines, jnp.stack([cosine_turns, sine_turns]))
    twist_real, twist_imag = rotation(
        spread_steps(row_count, column_count, turn_count), sequence_length, -1.0
    )
    section = rotate_pair(section, twist_real, twist_imag)
    section = contract("zfabk,zwaq->wfqbk", section, block_table(row_count, -1.0))
    cross_real, cross_imag = rotation(cross_steps(row_count, column_count), devices_all, -1.0)
    section = rotate_pair(section, cross_real, cross_imag)
    return contract("zfqbk,zwbr->wfqrk", section, block_table(column_count, -1.0))


def inverse_lines(spectrum, row_count, column_count):
    turn_count = spectrum.shape[-1]
    devices_all = row_count * column_count
    sequence_length = turn_count * devices_all
    section = contract("zfqrk,zwrb->wfqbk", spectrum, block_table(column_count, 1.0))
    cross_real, cross_imag = rotation(cross_steps(row_count, column_count), devices_all, 1.0)
    section = rotate_pair(section, cross_real, cross_imag)
    section = contract("zfqbk,zwqa->wfabk", section, block_table(row_count, 1.0))
    twist_real, twist_imag = rotation(
        spread_steps(row_count, column_count, turn_count), sequence_length, 1.0
    )
    section = rotate_pair(section, twist_real, twist_imag)
    cosine_turns, sine_turns = dft_table(turn_count, 1.0)
    result = contract("zfabk,zks->fabs", section, jnp.stack([cosine_turns, -sine_turns]))
    return result / sequence_length


def spectral_core(gated_grid, filter_grid, weighted_grid, row_count, column_count):
    turn_count = gated_grid.shape[-1]
    filter_factor = (turn_count * row_count * column_count) ** (-0.5)
    spectrum = forward_spectrum(
        jnp.stack([gated_grid, filter_grid, weighted_grid]), row_count, column_count
    )
    conv_part = times_pair(spectrum[:, 1], spectrum[:, 0], False)
    grad_part = times_pair(spectrum[:, 2], spectrum[:, 1], True)
    kernel_part = times_pair(spectrum[:, 2], spectrum[:, 0], True)
    joined = jnp.stack([conv_part, grad_part, kernel_part], axis=1)
    return inverse_lines(joined, row_count, column_count) * filter_factor


def on_device(projected, short_taps, long_filter, skip_gain, cotangent):
    channels = short_taps.shape[1]
    turn_count = projected.shape[-1]
    row_count = lax.axis_size("row")
    column_count = lax.axis_size("col")
    devices_all = row_count * column_count
    per_owner = channels // devices_all
    device_rank = lax.axis_index("row") * column_count + lax.axis_index("col")

    def shift_earlier(values):
        received = from_behind(values, ("row", "col"), 1)
        rolled = jnp.concatenate([jnp.zeros_like(received[..., :1]), received[..., :-1]], axis=-1)
        return jnp.where(device_rank == 0, rolled, received)

    def shift_later(values):
        received = from_behind(values, ("row", "col"), -1)
        rolled = jnp.concatenate([received[..., 1:], jnp.zeros_like(received[..., :1])], axis=-1)
        return jnp.where(device_rank == devices_all - 1, rolled, received)

    tap_zero = short_taps[:, :, 0:1]
    tap_one = short_taps[:, :, 1:2]
    tap_two = short_taps[:, :, 2:3]
    gain_column = skip_gain[:, None]
    projected_flat = projected.reshape(3, channels, turn_count)
    first_back = shift_earlier(projected_flat)
    second_back = shift_earlier(first_back)
    features = (
        tap_zero * projected_flat.astype(jnp.float32)
        + tap_one * first_back.astype(jnp.float32)
        + tap_two * second_back.astype(jnp.float32)
    )
    query_line = features[0]
    keys_line = features[1]
    values_line = features[2]
    gated_signal = keys_line * values_line
    seed_line = cotangent.reshape(channels, turn_count).astype(jnp.float32)
    weighted = query_line * seed_line
    filter_line = long_filter.reshape(channels, turn_count).astype(jnp.float32)
    values = jnp.stack([gated_signal, filter_line, weighted])
    outgoing = values.reshape(values.shape[0], row_count, column_count, per_owner, 1, 1, turn_count)
    arrived = lax.all_to_all(
        lax.all_to_all(outgoing, "row", split_axis=1, concat_axis=4, tiled=True),
        "col",
        split_axis=2,
        concat_axis=5,
        tiled=True,
    )

    def owner_spectra(item):
        return spectral_core(item[0], item[1], item[2], row_count, column_count)

    shaped = arrived.reshape(arrived.shape[0], per_owner, row_count, column_count, turn_count)
    results = lax.map(owner_spectra, jnp.moveaxis(shaped, 1, 0))
    moved = jnp.moveaxis(results, 0, 1)
    returned = lax.all_to_all(
        lax.all_to_all(
            moved.reshape(moved.shape[0], 1, 1, per_owner, row_count, column_count, turn_count),
            "row",
            split_axis=4,
            concat_axis=1,
            tiled=True,
        ),
        "col",
        split_axis=5,
        concat_axis=2,
        tiled=True,
    )
    lines = returned.reshape(returned.shape[0], channels, turn_count)
    convolved = lines[0]
    gated_back = lines[1]
    filter_grad = lines[2].astype(jnp.bfloat16)
    gated_grad = gated_back + gain_column * weighted
    mixed_inner = convolved + gain_column * gated_signal
    feature_grad = jnp.stack(
        [seed_line * mixed_inner, gated_grad * values_line, gated_grad * keys_line]
    ).astype(jnp.bfloat16)
    first_next = shift_later(feature_grad)
    second_next = shift_later(first_next)
    feature_back = lax.optimization_barrier(feature_grad).astype(jnp.float32)
    projected_grad = (
        tap_zero * feature_back
        + tap_one * first_next.astype(jnp.float32)
        + tap_two * second_next.astype(jnp.float32)
    ).astype(jnp.bfloat16)
    return (
        filter_grad.reshape(channels, 1, 1, turn_count),
        projected_grad.reshape(3, channels, 1, 1, turn_count),
    )


def solution(mesh):
    in_specs = (
        P(None, None, "row", "col", None),
        P(),
        P(None, "row", "col", None),
        P(),
        P(None, "row", "col", None),
    )
    out_specs = (P(None, "row", "col", None), P(None, None, "row", "col", None))
    return jax.shard_map(
        on_device, mesh=mesh, in_specs=in_specs, out_specs=out_specs, check_vma=False
    )
```

profile of v0, /device:TPU:1, one launch (start us, length us, event | category | flops | bytes accessed | tf_op | source)
XLA Modules:
  0.0 657.1 jit_solution(9288953874770834990)
XLA Ops:
  0.6 5.7 collective-permute-start
  6.3 44.7 %collective-permute-done = bf16[3,2048,128]{2,1,0:T(8,128)(2,1)S(1)} collective-permute-done((bf16[3,2048,128]{2,1,0:T(8,128)(2,1)}, bf16[3,2048,128]{2,1,0:T(8,128)(2,1)S(1)}, u32[]{:S(2)}, u32[]{:S(2)}) %collective-permute-start) | collective-permute-done | bytes 1572896 | tf_op jit(solution)/shard_map/ppermute | solution.py:11
  51.7 2.1 collective-permute-start.1
  54.1 39.6 %collective-permute-done.1 = bf16[3,2048,128]{2,1,0:T(8,128)(2,1)S(1)} collective-permute-done((bf16[3,2048,128]{2,1,0:T(8,128)(2,1)S(1)}, bf16[3,2048,128]{2,1,0:T(8,128)(2,1)S(1)}, u32[]{:S(2)}, u32[]{:S(2)}) %collective-permute-start.1) | collective-permute-done | bytes 1572896 | tf_op jit(solution)/shard_map/ppermute | solution.py:11
  93.7 3.3 multiply_add_fusion.7
  100.4 43.0 %all_to_all.66 = f32[3,16,32,4,1,1,128]{6,3,2,5,4,0,1:T(4,128)S(1)} all-to-all(f32[3,16,32,4,1,1,128]{6,3,2,5,4,0,1:T(4,128)S(1)} %copy.64), channel_id=1, replica_groups=mesh['row'=16,'col'=32] {'row'}, dimensions={1} | all-to-all | bytes 6291456 | tf_op jit(solution)/shard_map/all_to_all | solution.py:158
  143.4 2.6 copy.65
  146.0 7.4 %all-to-all-start.1 = ((f32[3,1,32,4,16,1,128]{6,3,4,0,5,1,2:T(4,128)}), f32[3,1,32,4,16,1,128]{6,3,4,0,5,1,2:T(4,128)}, u32[]{:S(2)}, u32[]{:S(2)}) async-start(f32[3,1,32,4,16,1,128]{6,3,4,0,5,1,2:T(4,128)} %copy.65), calls=%async_computation.1 | async-start | bytes 6291456 | tf_op jit(solution)/shard_map/all_to_all | solution.py:157
  153.4 139.9 %all-to-all-done.1 = f32[3,1,32,4,16,1,128]{6,3,4,0,5,1,2:T(4,128)} async-done(((f32[3,1,32,4,16,1,128]{6,3,4,0,5,1,2:T(4,128)}), f32[3,1,32,4,16,1,128]{6,3,4,0,5,1,2:T(4,128)}, u32[]{:S(2)}, u32[]{:S(2)}) %all-to-all-start.1) | async-done | bytes 3145760 | tf_op jit(solution)/shard_map/all_to_all | solution.py:157
  293.3 79.1 %while.13 = (s32[]{:T(128)}, f32[4,3,16,32,128]{4,3,1,0,2:T(8,128)}, f32[4,3,16,32,128]{4,0,2,1,3:T(4,128)}, s32[]{:T(128)}, s32[]{:T(128)}, /*index=5*/s32[]{}, s32[]{}) while((s32[]{:T(128)}, f32[4,3,16,32,128]{4,3,1,0,2:T(8,128)}, f32[4,3,16,32,128]{4,0,2,1,3:T(4,128)}, s32[]{:T(128)}, s32[]{:T(128)}, /*index=5*/s32[]{}, s32[]{}) %tuple.103), condition=%wide.region_1.2_spmd, body=%wide.region_0.1_spmd.sunk | while | flops 2124935680 | bytes 56972016 | solution.py:169
  293.3 2.7 constant_dynamic-slice_fusion.4
  300.0 2.3 fusion.144
  303.0 1.9 fusion.148
  305.3 1.5 fusion.149
  313.1 2.7 constant_dynamic-slice_fusion.4
  319.7 2.3 fusion.144
  322.8 1.9 fusion.148
  325.1 1.5 fusion.149
  332.9 2.7 constant_dynamic-slice_fusion.4
  339.5 2.3 fusion.144
  342.6 1.9 fusion.148
  352.7 2.7 constant_dynamic-slice_fusion.4
  359.3 2.3 fusion.144
  362.3 1.9 fusion.148
  372.4 47.8 %all_to_all.67 = f32[3,1,1,4,16,32,128]{6,5,0,3,2,1,4:T(8,128)S(1)} all-to-all(f32[3,1,1,4,16,32,128]{6,5,0,3,2,1,4:T(8,128)} %bitcast.67), channel_id=1, replica_groups=mesh['row'=16,'col'=32] {'row'}, dimensions={4} | all-to-all | bytes 6291456 | tf_op jit(solution)/shard_map/all_to_all | solution.py:172
  420.2 1.8 copy.68
  422.0 147.5 %all_to_all.68 = f32[3,16,1,4,1,32,128]{6,1,0,3,4,2,5:T(8,128)S(1)} all-to-all(f32[3,16,1,4,1,32,128]{6,1,0,3,4,2,5:T(8,128)S(1)} %copy.68), channel_id=1, replica_groups=mesh['row'=16,'col'=32] {'col'}, dimensions={5} | all-to-all | bytes 6291456 | tf_op jit(solution)/shard_map/all_to_all | solution.py:171
  573.8 3.2 collective-permute-start.2
  577.0 34.8 %collective-permute-done.2 = bf16[3,2048,128]{2,1,0:T(8,128)(2,1)S(1)} collective-permute-done((bf16[3,2048,128]{2,1,0:T(8,128)(2,1)S(1)}, bf16[3,2048,128]{2,1,0:T(8,128)(2,1)S(1)}, u32[]{:S(2)}, u32[]{:S(2)}) %collective-permute-start.2) | collective-permute-done | bytes 1572896 | tf_op jit(solution)/shard_map/ppermute | solution.py:11
  612.8 6.9 %collective-permute-start.3 = (bf16[3,2048,128]{2,1,0:T(8,128)(2,1)S(1)}, bf16[3,2048,128]{2,1,0:T(8,128)(2,1)S(1)}, u32[]{:S(2)}, u32[]{:S(2)}) collective-permute-start(bf16[3,2048,128]{2,1,0:T(8,128)(2,1)S(1)} %pad_select_fusion), channel_id=1, source_target_pairs={{0,511},{1,0},{2,1},{3,2},{4,3},{5,4},{6,5},{7,6},{8,7},{9,8},{10,... | collective-permute-start | bytes 4718600 | tf_op jit(solution)/shard_map/ppermute | solution.py:11
  622.1 29.9 %collective-permute-done.3 = bf16[3,2048,128]{2,1,0:T(8,128)(2,1)S(1)} collective-permute-done((bf16[3,2048,128]{2,1,0:T(8,128)(2,1)S(1)}, bf16[3,2048,128]{2,1,0:T(8,128)(2,1)S(1)}, u32[]{:S(2)}, u32[]{:S(2)}) %collective-permute-start.3) | collective-permute-done | bytes 1572896 | tf_op jit(solution)/shard_map/ppermute | solution.py:11
  652.5 4.6 fusion.100
  (183 shorter events, 60.1 us)
Async XLA Ops:
  0.6 50.3 %collective-permute-start = (bf16[3,2048,128]{2,1,0:T(8,128)(2,1)}, bf16[3,2048,128]{2,1,0:T(8,128)(2,1)S(1)}, u32[]{:S(2)}, u32[]{:S(2)}) collective-permute-start(bf16[3,2048,128]{2,1,0:T(8,128)(2,1)} %bitcast.308), channel_id=1, source_target_pairs={{0,1},{1,2},{2,3},{3,4},{4,5},{5,6},{6,7},{7,8},{8,9},{9,10},{10,1... | collective-permute-start | bytes 4718600 | tf_op jit(solution)/shard_map/ppermute | solution.py:11
  51.0 2.8 copy-start.11
  51.0 2.9 copy-start.10
  51.7 41.9 %copy-start.9 = (bf16[3,2048,1,1,128]{4,1,3,2,0:T(8,128)(2,1)S(1)}, bf16[3,2048,1,1,128]{4,1,3,2,0:T(8,128)(2,1)}, u32[]{:S(2)}) copy-start(bf16[3,2048,1,1,128]{4,1,3,2,0:T(8,128)(2,1)} %param.7) | copy-start | bytes 4718596
  51.7 41.9 %collective-permute-start.1 = (bf16[3,2048,128]{2,1,0:T(8,128)(2,1)S(1)}, bf16[3,2048,128]{2,1,0:T(8,128)(2,1)S(1)}, u32[]{:S(2)}, u32[]{:S(2)}) collective-permute-start(bf16[3,2048,128]{2,1,0:T(8,128)(2,1)S(1)} %pad_select_fusion.1), channel_id=1, source_target_pairs={{0,1},{1,2},{2,3},{3,4},{4,5},{5,6},{6,7},{7,8},{8,9},{9,10},{10,1... | collective-permute-start | bytes 4718600 | tf_op jit(solution)/shard_map/ppermute | solution.py:11
  93.7 3.3 copy-start.7
  97.3 1.0 copy-start.1
  97.3 1.3 copy-start.3
  146.0 147.3 %all-to-all-start.1 = ((f32[3,1,32,4,16,1,128]{6,3,4,0,5,1,2:T(4,128)}), f32[3,1,32,4,16,1,128]{6,3,4,0,5,1,2:T(4,128)}, u32[]{:S(2)}, u32[]{:S(2)}) async-start(f32[3,1,32,4,16,1,128]{6,3,4,0,5,1,2:T(4,128)} %copy.65), calls=%async_computation.1 | async-start | bytes 6291456 | tf_op jit(solution)/shard_map/all_to_all | solution.py:157
  569.5 1.6 copy-start
  571.1 1.0 copy-start.8
  571.1 1.0 copy-start.12
  571.5 1.3 copy-start.2
  571.6 1.6 copy-start.4
  573.8 3.2 copy-start.5
  573.8 38.0 %collective-permute-start.2 = (bf16[3,2048,128]{2,1,0:T(8,128)(2,1)S(1)}, bf16[3,2048,128]{2,1,0:T(8,128)(2,1)S(1)}, u32[]{:S(2)}, u32[]{:S(2)}) collective-permute-start(bf16[3,2048,128]{2,1,0:T(8,128)(2,1)S(1)} %pad_maximum_fusion.16), channel_id=1, source_target_pairs={{0,511},{1,0},{2,1},{3,2},{4,3},{5,4},{6,5},{7,6},{8,7},{9,8},{10,... | collective-permute-start | bytes 4718600 | tf_op jit(solution)/shard_map/ppermute | solution.py:11
  612.8 39.2 %collective-permute-start.3 = (bf16[3,2048,128]{2,1,0:T(8,128)(2,1)S(1)}, bf16[3,2048,128]{2,1,0:T(8,128)(2,1)S(1)}, u32[]{:S(2)}, u32[]{:S(2)}) collective-permute-start(bf16[3,2048,128]{2,1,0:T(8,128)(2,1)S(1)} %pad_select_fusion), channel_id=1, source_target_pairs={{0,511},{1,0},{2,1},{3,2},{4,3},{5,4},{6,5},{7,6},{8,7},{9,8},{10,... | collective-permute-start | bytes 4718600 | tf_op jit(solution)/shard_map/ppermute | solution.py:11
  622.1 30.4 %copy-start.6 = (bf16[3,2048,128]{2,1,0:T(8,128)(2,1)S(1)}, bf16[3,2048,128]{2,1,0:T(8,128)(2,1)}, u32[]{:S(2)}) copy-start(bf16[3,2048,128]{2,1,0:T(8,128)(2,1)} %copy-done.5) | copy-start | bytes 4718596
where the time goes:
time: 660 us; the launch traced here: 657 us
  waiting for transfers between devices  289 us (44%)
  blocking collectives  238 us (36%)
  matrix products  39.8 us (6%)
  other arithmetic  32.6 us (5%)
  local copies, waits for them, and re-layouts  30.5 us (5%)
  starting transfers between devices  25.2 us (4%)
    ppermute x4, waiting for transfers between devices, from_behind(): lax.ppermute(array, axis, [(i, (i + by) % devices) for i in range(devices)])  149 us
    all_to_all x1, blocking collectives, on_device(): lax.all_to_all(lax.all_to_all(moved.reshape(moved.shape[0], 1, 1, per_own...  148 us
    all_to_all x1, waiting for transfers between devices, on_device(): lax.all_to_all(lax.all_to_all(outgoing, 'row', split_axis=1, concat_axis=...  140 us
    all_to_all x1, blocking collectives, on_device(): lax.all_to_all(moved.reshape(moved.shape[0], 1, 1, per_owner, row_count,...  47.8 us
    all_to_all x1, blocking collectives, on_device(): lax.all_to_all(outgoing, 'row', split_axis=1, concat_axis=4, tiled=True)  43 us
    dot_general x24, matrix products, contract(): return jnp.einsum(form, left, right, precision=lax.Precision.HIGHEST)  39.8 us
    ppermute x4, starting transfers between devices, from_behind(): lax.ppermute(array, axis, [(i, (i + by) % devices) for i in range(devices)])  17.8 us
  transfers between devices with their start and end apart: 5, of which 5 were waited for; matrix products, arithmetic and copies ran while one was open for 0% of the time, Pallas kernels for 0%

commit v1 on v0

v1 whole, which is shorter than its diff:
```python
import math

import jax
import jax.numpy as jnp
import numpy as np
from jax import lax
from jax.sharding import PartitionSpec as P


def tables(turns, slots):
    length = turns * slots
    half = turns // 2 + 1
    k = np.arange(half)
    s = np.arange(turns)
    r = np.arange(slots)
    ang = 2.0 * math.pi * (np.outer(k, s) % turns) / turns
    first = np.concatenate([np.cos(ang), -np.sin(ang)], axis=0)
    weight = np.where((k == 0) | (k == turns // 2), 1.0, 2.0)[:, None]
    scale = 1.0 / length * length**-0.5
    last = np.concatenate([weight * np.cos(ang), weight * np.sin(ang)], axis=0) * scale
    ang = 2.0 * math.pi * np.outer(k, r) / length
    twist = (np.cos(ang).astype(np.float32), np.sin(ang).astype(np.float32))
    ang = 2.0 * math.pi * (np.outer(r, r) % slots) / slots
    c, sn = np.cos(ang), np.sin(ang)
    block = np.concatenate(
        [np.concatenate([c, -sn], axis=1), np.concatenate([sn, c], axis=1)], axis=0
    )
    return first, last, twist, block


def two(table):
    high = table.astype(np.float32).astype(jnp.bfloat16)
    low = (table - high.astype(np.float64)).astype(np.float32).astype(jnp.bfloat16)
    return jnp.asarray(high), jnp.asarray(low)


def parts_of(values):
    high = values.astype(jnp.bfloat16)
    low = (values - high.astype(jnp.float32)).astype(jnp.bfloat16)
    return high, low


def product(form, values, table):
    high, low = parts_of(values)
    t_high, t_low = table

    def one(left, right):
        return jnp.einsum(form, left, right, preferred_element_type=jnp.float32)

    return one(high, t_high) + (one(low, t_high) + one(high, t_low))


def earlier(lines):
    wrapped = jnp.pad(lines[..., -1:, :-1], [(0, 0)] * (lines.ndim - 1) + [(1, 0)])
    return jnp.concatenate([wrapped, lines[..., :-1, :]], axis=-2)


def later(lines):
    wrapped = jnp.pad(lines[..., :1, 1:], [(0, 0)] * (lines.ndim - 1) + [(0, 1)])
    return jnp.concatenate([lines[..., 1:, :], wrapped], axis=-2)


def owner(lines, taps, gain):
    slots, turns = lines.shape[-2:]
    half = turns // 2 + 1
    first, last, twist, block = tables(turns, slots)
    first, last, block = two(first), two(last), two(block)
    cos_t, sin_t = jnp.asarray(twist[0]), jnp.asarray(twist[1])
    taps = taps[..., None, None]
    gain = gain[:, None, None]
    lines = lines.astype(jnp.float32)
    raw = lines[:3]
    once = earlier(raw)
    features = taps[:, :, 0] * raw + taps[:, :, 1] * once + taps[:, :, 2] * earlier(once)
    query, keys, values = features[0], features[1], features[2]
    filt, seed = lines[3], lines[4]
    gated = keys * values
    weighted = query * seed
    spectra = product("fnrs,ks->fnkr", jnp.stack([gated, filt, weighted]), first)
    re, im = spectra[:, :, :half], spectra[:, :, half:]
    both = jnp.concatenate([re * cos_t + im * sin_t, im * cos_t - re * sin_t], axis=-1)
    both = product("fnkr,rq->fnkq", both, block)
    re, im = both[..., :slots], both[..., slots:]
    gr, fr, wr = re[0], re[1], re[2]
    gi, fi, wi = im[0], im[1], im[2]
    out_re = jnp.stack([gr * fr - gi * fi, wr * fr + wi * fi, wr * gr + wi * gi])
    neg_im = jnp.stack([-gr * fi - gi * fr, wr * fi - wi * fr, wr * gi - wi * gr])
    both = product("fnkq,qr->fnkr", jnp.concatenate([out_re, neg_im], axis=-1), block)
    re, nim = both[..., :slots], both[..., slots:]
    e_re = re * cos_t + nim * sin_t
    e_nim = nim * cos_t - re * sin_t
    lines = product("fnkr,ks->fnrs", jnp.concatenate([e_re, e_nim], axis=2), last)
    conv, back, filter_grad = lines[0], lines[1], lines[2]
    gated_grad = back + gain * weighted
    mixed = conv + gain * gated
    grads = jnp.stack([seed * mixed, gated_grad * values, gated_grad * keys]).astype(jnp.bfloat16)
    grads = lax.optimization_barrier(grads).astype(jnp.float32)
    once = later(grads)
    projected = taps[:, :, 0] * grads + taps[:, :, 1] * once + taps[:, :, 2] * later(once)
    return jnp.concatenate([projected, filter_grad[None]]).astype(jnp.bfloat16)


def on_device(projected, short_taps, long_filter, skip_gain, cotangent):
    channels = short_taps.shape[1]
    turns = projected.shape[-1]
    rows = lax.axis_size("row")
    cols = lax.axis_size("col")
    slots = rows * cols
    each = channels // slots
    rank = lax.axis_index("row") * cols + lax.axis_index("col")
    stacked = jnp.concatenate(
        [
            projected.reshape(3, channels, turns),
            long_filter.reshape(1, channels, turns),
            cotangent.reshape(1, channels, turns),
        ]
    )
    outgoing = stacked.reshape(5, rows, cols, each, 1, 1, turns)
    arrived = lax.all_to_all(
        lax.all_to_all(outgoing, "row", split_axis=1, concat_axis=4, tiled=True),
        "col",
        split_axis=2,
        concat_axis=5,
        tiled=True,
    )
    taps = lax.dynamic_slice_in_dim(short_taps, rank * each, each, 1)
    gain = lax.dynamic_slice_in_dim(skip_gain, rank * each, each, 0)
    results = owner(arrived.reshape(5, each, slots, turns), taps, gain)
    returned = lax.all_to_all(
        lax.all_to_all(
            results.reshape(4, 1, 1, each, rows, cols, turns),
            "col",
            split_axis=5,
            concat_axis=2,
            tiled=True,
        ),
        "row",
        split_axis=4,
        concat_axis=1,
        tiled=True,
    )
    lines = returned.reshape(4, channels, turns)
    return (
        lines[3].reshape(channels, 1, 1, turns),
        lines[:3].reshape(3, channels, 1, 1, turns),
    )


def solution(mesh):
    in_specs = (
        P(None, None, "row", "col", None),
        P(),
        P(None, "row", "col", None),
        P(),
        P(None, "row", "col", None),
    )
    out_specs = (P(None, "row", "col", None), P(None, None, "row", "col", None))
    return jax.shard_map(
        on_device, mesh=mesh, in_specs=in_specs, out_specs=out_specs, check_vma=False
    )
```

time: 660 us -> 371 us (0.56)
  waiting for transfers between devices: 289 us -> 116 us
  blocking collectives: 238 us -> 181 us
  other arithmetic: 32.6 us -> 10.4 us
  matrix products: 39.8 us -> 19.8 us
  starting transfers between devices: 25.2 us -> 15.2 us
  local copies, waits for them, and re-layouts: 30.5 us -> 22.3 us
    ppermute x4 -> x0, waiting for transfers between devices: 149 us -> none  [from_behind(): lax.ppermute(array, axis, [(i, (i + by) % devices) for i in range(devices)])]
    all_to_all x2, blocking collectives: 195 us -> 139 us  [the longest x1 107 us: on_device(): lax.all_to_all(results.reshape(4, 1, 1, each, rows, cols, turns), 'col',...]
    all_to_all x1, waiting for transfers between devices: 140 us -> 116 us  [on_device(): lax.all_to_all(lax.all_to_all(outgoing, 'row', split_axis=1, concat_axis=...]
    dot_general x24 -> x12, matrix products: 39.8 us -> 19.8 us  [one(): return jnp.einsum(form, left, right, preferred_element_type=jnp.float32)]
    ppermute x4 -> x0, starting transfers between devices: 17.8 us -> none  [from_behind(): lax.ppermute(array, axis, [(i, (i + by) % devices) for i in range(devices)])]
    all_to_all x1, starting transfers between devices: 7.38 us -> 15.2 us  [on_device(): lax.all_to_all(lax.all_to_all(outgoing, 'row', split_axis=1, concat_axis=...]
    slice x16 -> x17, local copies, waits for them, and re-layouts: 16 us -> 8.43 us  [the longest x3 2.47 us: owner(): raw = lines[:3]]
  transfers between devices with their start and end apart: 5 -> 1, of which waited for: 5 -> 1; matrix products, arithmetic and copies ran while one was open for 0% -> 0% of each run, Pallas kernels for 0% -> 0%
where the time goes in v1:
time: 371 us; the launch traced here: 367 us
  blocking collectives  181 us (49%)
  waiting for transfers between devices  116 us (31%)
  local copies, waits for them, and re-layouts  22.3 us (6%)
  matrix products  19.8 us (5%)
  starting transfers between devices  15.2 us (4%)
  other arithmetic  10.4 us (3%)
    all_to_all x1, waiting for transfers between devices, on_device(): lax.all_to_all(lax.all_to_all(outgoing, 'row', split_axis=1, concat_axis=...  116 us
    all_to_all x1, blocking collectives, on_device(): lax.all_to_all(results.reshape(4, 1, 1, each, rows, cols, turns), 'col',...  107 us
    all_to_all x1, blocking collectives, on_device(): lax.all_to_all(outgoing, 'row', split_axis=1, concat_axis=4, tiled=True)  41.8 us
    all_to_all x1, blocking collectives, on_device(): lax.all_to_all(lax.all_to_all(results.reshape(4, 1, 1, each, rows, cols,...  32.5 us
    dot_general x12, matrix products, one(): return jnp.einsum(form, left, right, preferred_element_type=jnp.float32)  19.8 us
    all_to_all x1, starting transfers between devices, on_device(): lax.all_to_all(lax.all_to_all(outgoing, 'row', split_axis=1, concat_axis=...  15.2 us
  transfers between devices with their start and end apart: 1, of which 1 were waited for; matrix products, arithmetic and copies ran while one was open for 0% of the time, Pallas kernels for 0%

profile of v1, /device:TPU:1, one launch (start us, length us, event | category | flops | bytes accessed | tf_op | source)
XLA Modules:
  0.0 366.5 jit_solution(9455076439806238314)
XLA Ops:
  0.6 3.9 %pad_maximum_fusion.3 = bf16[5,16,32,4,1,1,128]{6,3,2,1,0,5,4:T(4,128)(2,1)S(1)} fusion(bf16[1,16,32,4,1,1,128]{6,3,2,1,0,5,4:T(4,128)(2,1)} %bitcast.86, bf16[1,16,32,4,1,1,128]{6,3,2,1,0,5,4:T(4,128)(2,1)} %bitcast.87, bf16[3,16,32,4,1,1,128]{6,3,2,1,0,5,4:T(4,128)(2,1)} %bitcast.85), kind=kLoop, calls=%fused_computation.26 | loop fusion | flops 2621440 | bytes 5242880 | tf_op jit(solution)/shard_map/concatenate | solution.py:111
  4.5 0.7 copy.41
  5.3 41.8 %all_to_all.60 = bf16[5,16,32,4,1,1,128]{6,2,3,0,5,4,1:T(8,128)(2,1)S(1)} all-to-all(bf16[5,16,32,4,1,1,128]{6,2,3,0,5,4,1:T(8,128)(2,1)S(1)} %copy.41), channel_id=1, replica_groups=mesh['row'=16,'col'=32] {'row'}, dimensions={1} | all-to-all | bytes 5242880 | tf_op jit(solution)/shard_map/all_to_all | solution.py:120
  47.0 3.2 copy.42
  50.2 15.2 %all-to-all-start.1 = ((bf16[5,1,32,4,16,1,128]{6,4,3,0,5,1,2:T(8,128)(2,1)}), bf16[5,1,32,4,16,1,128]{6,4,3,0,5,1,2:T(8,128)(2,1)S(1)}, u32[]{:S(2)}, u32[]{:S(2)}) async-start(bf16[5,1,32,4,16,1,128]{6,4,3,0,5,1,2:T(8,128)(2,1)} %copy.42), calls=%async_computation.1 | async-start | bytes 5242880 | tf_op jit(solution)/shard_map/all_to_all | solution.py:119
  65.4 0.8 dynamic_slice.7
  66.5 116.4 %all-to-all-done.1 = bf16[5,1,32,4,16,1,128]{6,4,3,0,5,1,2:T(8,128)(2,1)S(1)} async-done(((bf16[5,1,32,4,16,1,128]{6,4,3,0,5,1,2:T(8,128)(2,1)}), bf16[5,1,32,4,16,1,128]{6,4,3,0,5,1,2:T(8,128)(2,1)S(1)}, u32[]{:S(2)}, u32[]{:S(2)}) %all-to-all-start.1) | async-done | bytes 2621472 | tf_op jit(solution)/shard_map/all_to_all | solution.py:119
  183.0 0.7 convert_bitcast_fusion
  183.9 2.0 copy-done.2
  185.9 3.0 copy.45
  191.1 1.8 copy.44
  193.2 1.3 fusion.4
  195.3 1.2 fusion.11
  196.5 1.2 fusion.33
  197.7 1.6 add_bitcast_fusion
  199.9 1.0 copy-done.10
  200.9 2.0 fusion.8
  202.9 2.0 fusion.17
  204.9 2.2 add_add_fusion.1
  208.0 2.0 fusion.9
  210.0 2.0 fusion.37
  212.0 2.2 add_add_fusion
  214.9 1.1 fusion.10
  216.0 1.3 fusion.21
  217.3 1.2 add_add_fusion.2
  218.6 0.7 multiply_convert_fusion.1
  220.6 0.9 fusion.2
  222.3 106.7 %all_to_all.61 = bf16[4,1,1,4,16,32,128]{6,4,3,0,2,1,5:T(8,128)(2,1)S(1)} all-to-all(bf16[4,1,1,4,16,32,128]{6,4,3,0,2,1,5:T(8,128)(2,1)S(1)} %pad_maximum_fusion.4), channel_id=1, replica_groups=mesh['row'=16,'col'=32] {'col'}, dimensions={5} | all-to-all | bytes 4194304 | tf_op jit(solution)/shard_map/all_to_all | solution.py:130
  329.1 1.4 copy.49
  330.4 32.5 %all_to_all.62 = bf16[4,1,32,4,16,1,128]{6,2,3,0,5,1,4:T(8,128)(2,1)S(1)} all-to-all(bf16[4,1,32,4,16,1,128]{6,2,3,0,5,1,4:T(8,128)(2,1)S(1)} %copy.49), channel_id=1, replica_groups=mesh['row'=16,'col'=32] {'row'}, dimensions={4} | all-to-all | bytes 4194304 | tf_op jit(solution)/shard_map/all_to_all | solution.py:129
  363.3 2.0 copy.51
  365.2 1.1 copy.50
  (47 shorter events, 8.4 us)
Async XLA Ops:
  0.6 65.6 %copy-start = (f32[3,2048,3]{1,2,0:T(4,128)S(1)}, f32[3,2048,3]{1,2,0:T(4,128)}, u32[]{:S(2)}) copy-start(f32[3,2048,3]{1,2,0:T(4,128)} %param.14) | copy-start | bytes 221188
  50.2 132.7 %all-to-all-start.1 = ((bf16[5,1,32,4,16,1,128]{6,4,3,0,5,1,2:T(8,128)(2,1)}), bf16[5,1,32,4,16,1,128]{6,4,3,0,5,1,2:T(8,128)(2,1)S(1)}, u32[]{:S(2)}, u32[]{:S(2)}) async-start(bf16[5,1,32,4,16,1,128]{6,4,3,0,5,1,2:T(8,128)(2,1)} %copy.42), calls=%async_computation.1 | async-start | bytes 5242880 | tf_op jit(solution)/shard_map/all_to_all | solution.py:119
  183.6 2.3 copy-start.2
  189.2 1.9 slice-start
  194.5 0.8 copy-start.6
  196.5 1.2 copy-start.9
  197.7 1.6 copy-start.4
  197.7 1.6 copy-start.5
  199.3 1.6 copy-start.10
  202.9 2.0 copy-start.3
  214.2 0.8 copy-start.8
  216.0 1.3 copy-start.7
  362.9 3.4 copy-start.1

commit v2 on v1

v2 whole, which is shorter than its diff:
```python
import functools
import math

import jax
import jax.numpy as jnp
import numpy as np
from jax import lax
from jax.experimental import pallas as pl
from jax.experimental.pallas import tpu as pltpu
from jax.sharding import PartitionSpec as P

MESH = pl.DeviceIdType.MESH
BF16 = jnp.bfloat16
F32 = jnp.float32
PAD = 80


def two(table):
    high = table.astype(np.float32).astype(BF16)
    low = (table - high.astype(np.float64)).astype(np.float32).astype(BF16)
    return np.stack([high, low])


def tables(turns, planes, depth):
    slots = planes * depth
    length = turns * slots
    half = turns // 2 + 1
    z, g = np.meshgrid(np.arange(depth), np.arange(planes), indexing="ij")
    r = ((g // 2) * 2 * depth + z * 2 + g % 2).reshape(-1)
    k = np.arange(half)
    angles = 2.0 * math.pi * (np.outer(k, np.arange(turns)) % turns) / turns
    weight = np.where((k == 0) | (k == turns // 2), 1.0, 2.0)[:, None]
    scale = 1.0 / length * length**-0.5

    def padded(table):
        return np.pad(table, [(0, PAD - half), (0, 0)])

    cosine, sine = padded(np.cos(angles)), padded(np.sin(angles))
    first = np.concatenate([cosine, -sine])
    weight = padded(weight) * scale
    last = np.concatenate([weight * cosine, weight * sine]).T
    angles = 2.0 * math.pi * np.outer(k, r) / length
    twist = np.stack([padded(np.cos(angles)), padded(np.sin(angles))]).astype(np.float32)
    angles = 2.0 * math.pi * (np.outer(r, r) % slots) / slots
    cosine, sine = np.cos(angles), np.sin(angles)
    block = np.block([[cosine, -sine], [sine, cosine]])
    return two(first), two(last), twist, two(block)


def split(values):
    high = values.astype(BF16)
    return high, (values - high.astype(F32)).astype(BF16)


def dot(left, right):
    return jnp.dot(left, right, preferred_element_type=F32)


def dot_t(left, right):
    return lax.dot_general(left, right, (((1,), (1,)), ((), ())), preferred_element_type=F32)


def kernel(
    planes,
    depth,
    scalars,
    projected,
    filt,
    cotangent,
    first_hbm,
    last_hbm,
    twist_hbm,
    block_hbm,
    filter_out,
    projected_out,
    held,
    arrived1,
    leaving2,
    arrived2,
    leaving3,
    arrived3,
    leaving4,
    arrived4,
    first,
    last,
    twist,
    block,
    flat,
    lines,
    spectra,
    factors,
    load_sem,
    table_sem,
    send_sem,
    recv_sem,
    out_sem,
):
    chunks = held.shape[0]
    turns = held.shape[-1]
    slots = planes * depth
    row = lax.axis_index("row")
    col = lax.axis_index("col")
    z = col // 2
    g = row * 2 + col % 2

    def at_plane(step):
        peer = lax.rem(g + step, planes)
        return peer, (peer // 2, z * 2 + lax.rem(peer, 2))

    def at_depth(step):
        away = (1 - 2 * lax.rem(step, 2)) * (step // 2 + 1)
        peer = lax.rem(z + away + depth, depth)
        return peer, (row, peer * 2 + lax.rem(col, 2))

    def await_bytes(ref, sem):
        pltpu.make_async_copy(ref, ref, sem).wait()

    def load_copies(j):
        rows = pl.ds(j * slots, slots)
        return (
            pltpu.make_async_copy(
                projected.at[:, rows], held.at[j, pl.ds(0, 3)], load_sem.at[j, 0]
            ),
            pltpu.make_async_copy(filt.at[rows], held.at[j, 3], load_sem.at[j, 1]),
            pltpu.make_async_copy(cotangent.at[rows], held.at[j, 4], load_sem.at[j, 2]),
        )

    def table_copies():
        return (
            pltpu.make_async_copy(first_hbm, first, table_sem.at[0]),
            pltpu.make_async_copy(last_hbm, last, table_sem.at[1]),
            pltpu.make_async_copy(twist_hbm, twist, table_sem.at[2]),
            pltpu.make_async_copy(block_hbm, block, table_sem.at[3]),
        )

    def out_copies(j):
        rows = pl.ds(j * slots, slots)
        return (
            pltpu.make_async_copy(
                arrived4.at[j, pl.ds(0, 3)], projected_out.at[:, rows], out_sem.at[j, 0]
            ),
            pltpu.make_async_copy(arrived4.at[j, 3], filter_out.at[rows], out_sem.at[j, 1]),
        )

    def loop(count, body):
        lax.fori_loop(0, count, lambda i, carry: (body(i), carry)[1], 0)

    for j in range(chunks):
        for copy in load_copies(j):
            copy.start()
    for copy in table_copies():
        copy.start()

    barrier = pltpu.get_barrier_semaphore()

    def greet_plane(i):
        _, device = at_plane(i + 1)
        pl.semaphore_signal(barrier, inc=1, device_id=device, device_id_type=MESH)

    def greet_depth(i):
        _, device = at_depth(i)
        pl.semaphore_signal(barrier, inc=1, device_id=device, device_id_type=MESH)

    loop(planes - 1, greet_plane)
    loop(depth - 1, greet_depth)
    pl.semaphore_wait(barrier, planes + depth - 2)

    def send_all(phase, j, count, at, own, source, target):
        pltpu.make_async_copy(source(own), target(own), recv_sem.at[phase, j]).start()

        def one(i):
            peer, device = at(i)
            pltpu.make_async_remote_copy(
                src_ref=source(peer),
                dst_ref=target(own),
                send_sem=send_sem.at[phase, j],
                recv_sem=recv_sem.at[phase, j],
                device_id=device,
                device_id_type=MESH,
            ).start()

        loop(count - 1, one)

    def next_plane(i):
        return at_plane(i + 1)

    def enter(j):
        for copy in load_copies(j):
            copy.wait()
        send_all(
            0,
            j,
            planes,
            next_plane,
            g,
            lambda peer: held.at[j, :, pl.ds(pl.multiple_of(peer * depth, depth), depth)],
            lambda own: arrived1.at[j, own],
        )

    loop(chunks, enter)

    def pass_on(j):
        await_bytes(arrived1.at[j], recv_sem.at[0, j])

        def sort(i):
            flat[...] = arrived1[j, :, i].astype(F32).reshape(slots, turns)
            for peer in range(depth):
                leaving2[j, peer, i] = flat[pl.ds(peer, planes, stride=depth), :].astype(BF16)

        loop(5, sort)
        send_all(
            1,
            j,
            depth,
            at_depth,
            z,
            lambda peer: leaving2.at[j, peer],
            lambda own: arrived2.at[j, own],
        )

    loop(chunks, pass_on)

    for copy in table_copies():
        copy.wait()

    row_of = lax.broadcasted_iota(jnp.int32, (slots, turns), 0)
    odd = lax.rem(row_of, 2) == 1
    edge_row = lax.broadcasted_iota(jnp.int32, (planes, turns), 0)
    edge_lane = lax.broadcasted_iota(jnp.int32, (planes, turns), 1)

    def earlier(now):
        edge = pltpu.roll(now[slots - planes :], 2, 0)
        wrapped = jnp.where(edge_lane == 0, 0.0, pltpu.roll(edge, 1, 1))
        edge = jnp.where(edge_row < 2, wrapped, edge)
        second = jnp.concatenate([edge, now[: slots - planes]], axis=0)
        return jnp.where(odd, pltpu.roll(now, 1, 0), pltpu.roll(second, slots - 1, 0)), second

    def later(now):
        edge = pltpu.roll(now[:planes], planes - 2, 0)
        wrapped = jnp.where(edge_lane == turns - 1, 0.0, pltpu.roll(edge, turns - 1, 1))
        edge = jnp.where(edge_row >= planes - 2, wrapped, edge)
        second = jnp.concatenate([now[planes:], edge], axis=0)
        return jnp.where(odd, pltpu.roll(second, 1, 0), pltpu.roll(now, slots - 1, 0)), second

    def transform():
        width = min(256, 2 * slots)

        def columns(i):
            at = pl.ds(pl.multiple_of(i * width, width), width)
            high, low = factors[0], factors[1]
            spectra[:, at] = dot(high, block[0, :, at]) + (
                dot(low, block[0, :, at]) + dot(high, block[1, :, at])
            )

        loop(2 * slots // width, columns)

    def put(i, real, imag):
        rows = pl.ds(i * PAD, PAD)
        for side, part in ((0, real), (slots, imag)):
            high, low = split(part)
            factors[0, rows, pl.ds(side, slots)] = high
            factors[1, rows, pl.ds(side, slots)] = low

    def get(i):
        rows = pl.ds(i * PAD, PAD)
        return spectra[rows, pl.ds(0, slots)], spectra[rows, pl.ds(slots, slots)]

    def own_channel(j):
        await_bytes(arrived2.at[j], recv_sem.at[1, j])

        def line(i):
            return arrived2[j, :, i].astype(F32).reshape(slots, turns)

        def feature(i):
            now = line(i)
            first_back, second_back = earlier(now)
            return (
                scalars[j * 10 + i * 3] * now
                + scalars[j * 10 + i * 3 + 1] * first_back
                + scalars[j * 10 + i * 3 + 2] * second_back
            )

        lines[0] = feature(1)
        lines[1] = feature(2)
        lines[2] = lines[0] * lines[1]
        lines[3] = line(3)
        lines[4] = feature(0) * line(4)

        def spectrum(i):
            high, low = split(lines[2 + i])
            turned = dot_t(first[0], high) + (dot_t(first[0], low) + dot_t(first[1], high))
            real, imag = turned[:PAD], turned[PAD:]
            put(i, real * twist[0] + imag * twist[1], imag * twist[0] - real * twist[1])

        for i in range(3):
            spectrum(i)
        transform()
        gated_re, gated_im = get(0)
        filt_re, filt_im = get(1)
        put(
            0,
            gated_re * filt_re - gated_im * filt_im,
            -(gated_re * filt_im) - gated_im * filt_re,
        )
        gated_re, gated_im = get(0)
        filt_re, filt_im = get(1)
        side_re, side_im = get(2)
        put(
            1,
            side_re * filt_re + side_im * filt_im,
            side_re * filt_im - side_im * filt_re,
        )
        put(
            2,
            side_re * gated_re + side_im * gated_im,
            side_re * gated_im - side_im * gated_re,
        )
        transform()

        def back(i):
            real, imag = get(i)
            turned = jnp.concatenate(
                [real * twist[0] + imag * twist[1], imag * twist[0] - real * twist[1]], axis=0
            )
            high, low = split(turned)
            result = dot(last[0], high) + (dot(last[0], low) + dot(last[1], high))
            return jnp.transpose(result)

        gain = scalars[j * 10 + 9]
        lines[2] = back(0) + gain * lines[2]
        lines[4] = back(1) + gain * lines[4]
        leaving3[j, :, 3] = back(2).astype(BF16).reshape(depth, planes, turns)

        def leave(i, grad):
            now = grad.astype(BF16).astype(F32)
            first_next, second_next = later(now)
            total = (
                scalars[j * 10 + i * 3] * now
                + scalars[j * 10 + i * 3 + 1] * first_next
                + scalars[j * 10 + i * 3 + 2] * second_next
            )
            leaving3[j, :, i] = total.astype(BF16).reshape(depth, planes, turns)

        leave(0, line(4) * lines[2])
        leave(1, lines[4] * lines[1])
        leave(2, lines[4] * lines[0])
        send_all(
            2,
            j,
            depth,
            at_depth,
            z,
            lambda peer: leaving3.at[j, peer],
            lambda own: arrived3.at[j, own],
        )

    loop(chunks, own_channel)

    def hand_back(j):
        await_bytes(arrived3.at[j], recv_sem.at[2, j])

        def sort(i):
            flat[...] = arrived3[j, :, i].astype(F32).reshape(slots, turns)
            for peer in range(planes):
                leaving4[j, peer, i] = flat[pl.ds(peer, depth, stride=planes), :].astype(BF16)

        loop(4, sort)
        send_all(
            3,
            j,
            planes,
            next_plane,
            g,
            lambda peer: leaving4.at[j, peer],
            lambda own: arrived4.at[j, :, pl.ds(pl.multiple_of(own * depth, depth), depth)],
        )

    loop(chunks, hand_back)

    def finish(j):
        await_bytes(arrived4.at[j], recv_sem.at[3, j])
        for copy in out_copies(j):
            copy.start()

    loop(chunks, finish)

    def close(j):
        for copy in out_copies(j):
            copy.wait()
        await_bytes(held.at[j, :, pl.ds(0, (planes - 1) * depth)], send_sem.at[0, j])
        await_bytes(leaving2.at[j, pl.ds(0, depth - 1)], send_sem.at[1, j])
        await_bytes(leaving3.at[j, pl.ds(0, depth - 1)], send_sem.at[2, j])
        await_bytes(leaving4.at[j, pl.ds(0, planes - 1)], send_sem.at[3, j])

    loop(chunks, close)


def on_device(projected, short_taps, long_filter, skip_gain, cotangent):
    channels = short_taps.shape[1]
    turns = projected.shape[-1]
    rows = lax.axis_size("row")
    depth = lax.axis_size("col") // 2
    planes = rows * 2
    slots = planes * depth
    chunks = channels // slots
    col = lax.axis_index("col")
    place = (lax.axis_index("row") * 2 + col % 2) * depth + col // 2
    taps = lax.dynamic_slice_in_dim(
        short_taps.reshape(3, chunks, slots, 3), place, 1, 2
    ).reshape(3, chunks, 3)
    gain = lax.dynamic_slice_in_dim(skip_gain.reshape(chunks, slots), place, 1, 1)
    scalars = jnp.concatenate(
        [jnp.swapaxes(taps, 0, 1).reshape(chunks, 9), gain], axis=1
    ).reshape(-1)
    made = [jnp.asarray(t) for t in tables(turns, planes, depth)]
    anywhere = pl.BlockSpec(memory_space=pl.ANY)

    def vmem(*shape, dtype=BF16):
        return pltpu.VMEM(shape, dtype)

    filter_grad, projected_grad = pl.pallas_call(
        functools.partial(kernel, planes, depth),
        out_shape=(
            jax.ShapeDtypeStruct((channels, turns), BF16),
            jax.ShapeDtypeStruct((3, channels, turns), BF16),
        ),
        in_specs=[pl.BlockSpec(memory_space=pltpu.SMEM)] + [anywhere] * 7,
        out_specs=(anywhere, anywhere),
        scratch_shapes=[
            vmem(chunks, 5, slots, turns),
            vmem(chunks, planes, 5, depth, turns),
            vmem(chunks, depth, 5, planes, turns),
            vmem(chunks, depth, 5, planes, turns),
            vmem(chunks, depth, 4, planes, turns),
            vmem(chunks, depth, 4, planes, turns),
            vmem(chunks, planes, 4, depth, turns),
            vmem(chunks, 4, slots, turns),
            *[pltpu.VMEM(t.shape, t.dtype) for t in made],
            vmem(slots, turns, dtype=F32),
            vmem(5, slots, turns, dtype=F32),
            vmem(3 * PAD, 2 * slots, dtype=F32),
            vmem(2, 3 * PAD, 2 * slots),
            pltpu.SemaphoreType.DMA((chunks, 3)),
            pltpu.SemaphoreType.DMA((4,)),
            pltpu.SemaphoreType.DMA((4, chunks)),
            pltpu.SemaphoreType.DMA((4, chunks)),
            pltpu.SemaphoreType.DMA((chunks, 2)),
        ],
        compiler_params=pltpu.CompilerParams(
            collective_id=0, has_side_effects=True, vmem_limit_bytes=56 << 20
        ),
    )(
        scalars,
        projected.reshape(3, channels, turns),
        long_filter.reshape(channels, turns),
        cotangent.reshape(channels, turns),
        *made,
    )
    return (
        filter_grad.reshape(channels, 1, 1, turns),
        projected_grad.reshape(3, channels, 1, 1, turns),
    )


def solution(mesh):
    in_specs = (
        P(None, None, "row", "col", None),
        P(),
        P(None, "row", "col", None),
        P(),
        P(None, "row", "col", None),
    )
    out_specs = (P(None, "row", "col", None), P(None, None, "row", "col", None))
    return jax.shard_map(
        on_device, mesh=mesh, in_specs=in_specs, out_specs=out_specs, check_vma=False
    )
```

time: 371 us -> 255 us (0.69)
  Pallas kernels: 0 us -> 243 us
  blocking collectives: 181 us -> 0 us
  waiting for transfers between devices: 116 us -> 0 us
  matrix products: 19.8 us -> 0 us
  starting transfers between devices: 15.2 us -> 0 us
  local copies, waits for them, and re-layouts: 22.3 us -> 7.21 us
  other arithmetic: 10.4 us -> 0.08 us
    pallas_call x0 -> x1, Pallas kernels: none -> 243 us  [on_device(): pl.pallas_call(functools.partial(kernel, planes, depth), out_shape=(jax.S...]
    all_to_all x3 -> x0, blocking collectives: 181 us -> none  [the longest x1 107 us: on_device(): lax.all_to_all(results.reshape(4, 1, 1, each, rows, cols, turns), 'col',...]
    all_to_all x1 -> x0, waiting for transfers between devices: 116 us -> none  [on_device(): lax.all_to_all(lax.all_to_all(outgoing, 'row', split_axis=1, concat_axis=...]
    dot_general x12 -> x0, matrix products: 19.8 us -> none  [one(): return jnp.einsum(form, left, right, preferred_element_type=jnp.float32)]
    all_to_all x1 -> x0, starting transfers between devices: 15.2 us -> none  [on_device(): lax.all_to_all(lax.all_to_all(outgoing, 'row', split_axis=1, concat_axis=...]
    slice x17 -> x0, local copies, waits for them, and re-layouts: 8.43 us -> none  [the longest x3 2.47 us: owner(): raw = lines[:3]]
    all_to_all x2 -> x0, local copies, waits for them, and re-layouts: 4.54 us -> none  [the longest x1 3.18 us: on_device(): lax.all_to_all(outgoing, 'row', split_axis=1, concat_axis=4, tiled=True)]
    concatenate x4 -> x1, other arithmetic: 4.56 us -> 0.08 us  [on_device(): jnp.concatenate([jnp.swapaxes(taps, 0, 1).reshape(chunks, 9), gain], axis=1)]
  transfers between devices with their start and end apart: 1 -> 0, of which waited for: 1 -> 0; matrix products, arithmetic and copies ran while one was open for 0% -> 0% of each run, Pallas kernels for 0% -> 0%
where the time goes in v2:
time: 255 us; the launch traced here: 251 us
  Pallas kernels  243 us (95%)
  local copies, waits for them, and re-layouts  7.21 us (3%)
    pallas_call x1, Pallas kernels, on_device(): pl.pallas_call(functools.partial(kernel, planes, depth), out_shape=(jax.S...  243 us

profile of v2, /device:TPU:1, one launch (start us, length us, event | category | flops | bytes accessed | tf_op | source)
XLA Modules:
  0.0 250.8 jit_solution(6039524256877573485)
XLA Ops:
  0.7 0.7 reshape.37
  1.4 0.1 constant_dynamic-slice_fusion
  1.4 1.0 reshape.34
  2.4 0.1 constant_dynamic-slice_fusion.1
  2.5 0.2 copy.18
  2.7 0.1 reshape.36
  2.8 0.1 pad_maximum_fusion
  2.8 0.6 reshape.38.scalars
  3.4 242.9 %shard_map.104 = (bf16[2048,128]{1,0:T(8,128)(2,1)}, bf16[3,2048,128]{2,1,0:T(8,128)(2,1)}) custom-call(f32[40]{0:T(128)} %reshape.38.scalars, bf16[3,2048,128]{2,1,0:T(8,128)(2,1)} %bitcast.14, bf16[2048,128]{1,0:T(8,128)(2,1)} %bitcast.16, bf16[2048,128]{1,0:T(8,128)(2,1)} %bitcast.17, bf16[2,160,128]{2,1,0:T(8,128)(2,1)} %constant.46.clone.first_hbm, ...), custom_call_target="tpu_custom_call" | custom-call | tf_op jit(solution)/shard_map/pallas_call | solution.py:421
  246.3 1.9 copy.21
  248.2 2.7 %copy.22 = bf16[3,2048,1,1,128]{4,1,3,2,0:T(8,128)(2,1)} copy(bf16[3,2048,1,1,128]{4,1,3,2,0:T(8,128)(2,1)} %bitcast.13) | data formatting | bytes 3145728

commit v3 on v2

--- a/solution.py
+++ b/solution.py
@@ -63,7 +63,8 @@
 def kernel(
     planes,
     depth,
-    scalars,
+    taps_hbm,
+    gains_hbm,
     projected,
     filt,
     cotangent,
@@ -74,13 +75,15 @@
     filter_out,
     projected_out,
     held,
-    arrived1,
-    leaving2,
-    arrived2,
-    leaving3,
-    arrived3,
-    leaving4,
-    arrived4,
+    own_in,
+    leaving_in,
+    arrived_in,
+    own_out,
+    leaving_out,
+    arrived_out,
+    returned,
+    taps,
+    gains,
     first,
     last,
     twist,
@@ -101,10 +104,10 @@
     row = lax.axis_index("row")
     col = lax.axis_index("col")
     z = col // 2
-    g = row * 2 + col % 2
+    g = row * 2 + lax.rem(col, 2)
 
     def at_plane(step):
-        peer = lax.rem(g + step, planes)
+        peer = lax.rem(g + step + 1, planes)
         return peer, (peer // 2, z * 2 + lax.rem(peer, 2))
 
     def at_depth(step):
@@ -126,20 +129,26 @@
         )
 
     def table_copies():
-        return (
-            pltpu.make_async_copy(first_hbm, first, table_sem.at[0]),
-            pltpu.make_async_copy(last_hbm, last, table_sem.at[1]),
-            pltpu.make_async_copy(twist_hbm, twist, table_sem.at[2]),
-            pltpu.make_async_copy(block_hbm, block, table_sem.at[3]),
-        )
+        pairs = (
+            (taps_hbm, taps),
+            (gains_hbm, gains),
+            (first_hbm, first),
+            (last_hbm, last),
+            (twist_hbm, twist),
+            (block_hbm, block),
+        )
+        return [
+            pltpu.make_async_copy(source, target, table_sem.at[i])
+            for i, (source, target) in enumerate(pairs)
+        ]
 
     def out_copies(j):
         rows = pl.ds(j * slots, slots)
         return (
             pltpu.make_async_copy(
-                arrived4.at[j, pl.ds(0, 3)], projected_out.at[:, rows], out_sem.at[j, 0]
+                returned.at[j, pl.ds(0, 3)], projected_out.at[:, rows], out_sem.at[j, 0]
             ),
-            pltpu.make_async_copy(arrived4.at[j, 3], filter_out.at[rows], out_sem.at[j, 1]),
+            pltpu.make_async_copy(returned.at[j, 3], filter_out.at[rows], out_sem.at[j, 1]),
         )
 
     def loop(count, body):
@@ -153,19 +162,19 @@
 
     barrier = pltpu.get_barrier_semaphore()
 
-    def greet_plane(i):
-        _, device = at_plane(i + 1)
-        pl.semaphore_signal(barrier, inc=1, device_id=device, device_id_type=MESH)
-
-    def greet_depth(i):
-        _, device = at_depth(i)
-        pl.semaphore_signal(barrier, inc=1, device_id=device, device_id_type=MESH)
-
-    loop(planes - 1, greet_plane)
-    loop(depth - 1, greet_depth)
+    def greet(at):
+        def one(i):
+            _, device = at(i)
+            pl.semaphore_signal(barrier, inc=1, device_id=device, device_id_type=MESH)
+
+        return one
+
+    loop(depth - 1, greet(at_depth))
+    loop(planes - 1, greet(at_plane))
     pl.semaphore_wait(barrier, planes + depth - 2)
 
-    def send_all(phase, j, count, at, own, source, target):
+    def send_all(phase, j, source, target):
+        count, at, own = (depth, at_depth, z) if phase in (0, 3) else (planes, at_plane, g)
         pltpu.make_async_copy(source(own), target(own), recv_sem.at[phase, j]).start()
 
         def one(i):
@@ -181,8 +190,15 @@
 
         loop(count - 1, one)
 
-    def next_plane(i):
-        return at_plane(i + 1)
+    def exchange(source, target, j):
+        outer, arrays, inner = source.shape[1:4]
+
+        def one(i):
+            flat[...] = source[j, :, i].astype(F32).reshape(slots, turns)
+            for k in range(inner):
+                target[j, k, i] = flat[pl.ds(k, outer, stride=inner), :].astype(BF16)
+
+        loop(arrays, one)
 
     def enter(j):
         for copy in load_copies(j):
@@ -190,36 +206,11 @@
         send_all(
             0,
             j,
-            planes,
-            next_plane,
-            g,
-            lambda peer: held.at[j, :, pl.ds(pl.multiple_of(peer * depth, depth), depth)],
-            lambda own: arrived1.at[j, own],
+            lambda peer: held.at[j, :, pl.ds(pl.multiple_of(peer * planes, planes), planes)],
+            lambda own: own_in.at[j, own],
         )
 
     loop(chunks, enter)
-
-    def pass_on(j):
-        await_bytes(arrived1.at[j], recv_sem.at[0, j])
-
-        def sort(i):
-            flat[...] = arrived1[j, :, i].astype(F32).reshape(slots, turns)
-            for peer in range(depth):
-                leaving2[j, peer, i] = flat[pl.ds(peer, planes, stride=depth), :].astype(BF16)
-
-        loop(5, sort)
-        send_all(
-            1,
-            j,
-            depth,
-            at_depth,
-            z,
-            lambda peer: leaving2.at[j, peer],
-            lambda own: arrived2.at[j, own],
-        )
-
-    loop(chunks, pass_on)
-
     for copy in table_copies():
         copy.wait()
 
@@ -266,18 +257,31 @@
         return spectra[rows, pl.ds(0, slots)], spectra[rows, pl.ds(slots, slots)]
 
     def own_channel(j):
-        await_bytes(arrived2.at[j], recv_sem.at[1, j])
+        await_bytes(own_in.at[j], recv_sem.at[0, j])
+        exchange(own_in, leaving_in, j)
+        send_all(1, j, lambda peer: leaving_in.at[j, peer], lambda own: arrived_in.at[j, own])
+        await_bytes(arrived_in.at[j], recv_sem.at[1, j])
+        exchange(arrived_in, own_in, j)
+
+        mine = pl.ds(pl.multiple_of(j * slots, slots), slots)
+        here = lax.broadcasted_iota(jnp.int32, (1, slots), 1) == z * planes + g
+
+        def pick(values):
+            return jnp.sum(jnp.where(here, values, 0.0), axis=1, keepdims=True)
+
+        tap = [[pick(taps[i, pl.ds(t, 1), mine]) for t in range(3)] for i in range(3)]
+        gain = pick(gains[:, mine])
 
         def line(i):
-            return arrived2[j, :, i].astype(F32).reshape(slots, turns)
+            return own_in[j, :, i].astype(F32).reshape(slots, turns)
 
         def feature(i):
             now = line(i)
             first_back, second_back = earlier(now)
             return (
-                scalars[j * 10 + i * 3] * now
-                + scalars[j * 10 + i * 3 + 1] * first_back
-                + scalars[j * 10 + i * 3 + 2] * second_back
+                tap[i][0] * now
+                + tap[i][1] * first_back
+                + tap[i][2] * second_back
             )
 
         lines[0] = feature(1)
@@ -326,59 +330,38 @@
             result = dot(last[0], high) + (dot(last[0], low) + dot(last[1], high))
             return jnp.transpose(result)
 
-        gain = scalars[j * 10 + 9]
         lines[2] = back(0) + gain * lines[2]
         lines[4] = back(1) + gain * lines[4]
-        leaving3[j, :, 3] = back(2).astype(BF16).reshape(depth, planes, turns)
+        own_out[j, :, 3] = back(2).astype(BF16).reshape(depth, planes, turns)
 
         def leave(i, grad):
             now = grad.astype(BF16).astype(F32)
             first_next, second_next = later(now)
             total = (
-                scalars[j * 10 + i * 3] * now
-                + scalars[j * 10 + i * 3 + 1] * first_next
-                + scalars[j * 10 + i * 3 + 2] * second_next
+                tap[i][0] * now
+                + tap[i][1] * first_next
+                + tap[i][2] * second_next
             )
-            leaving3[j, :, i] = total.astype(BF16).reshape(depth, planes, turns)
+            own_out[j, :, i] = total.astype(BF16).reshape(depth, planes, turns)
 
         leave(0, line(4) * lines[2])
         leave(1, lines[4] * lines[1])
         leave(2, lines[4] * lines[0])
-        send_all(
-            2,
-            j,
-            depth,
-            at_depth,
-            z,
-            lambda peer: leaving3.at[j, peer],
-            lambda own: arrived3.at[j, own],
-        )
-
-    loop(chunks, own_channel)
-
-    def hand_back(j):
-        await_bytes(arrived3.at[j], recv_sem.at[2, j])
-
-        def sort(i):
-            flat[...] = arrived3[j, :, i].astype(F32).reshape(slots, turns)
-            for peer in range(planes):
-                leaving4[j, peer, i] = flat[pl.ds(peer, depth, stride=planes), :].astype(BF16)
-
-        loop(4, sort)
+        exchange(own_out, leaving_out, j)
+        send_all(2, j, lambda peer: leaving_out.at[j, peer], lambda own: arrived_out.at[j, own])
+        await_bytes(arrived_out.at[j], recv_sem.at[2, j])
+        exchange(arrived_out, own_out, j)
         send_all(
             3,
             j,
-            planes,
-            next_plane,
-            g,
-            lambda peer: leaving4.at[j, peer],
-            lambda own: arrived4.at[j, :, pl.ds(pl.multiple_of(own * depth, depth), depth)],
-        )
-
-    loop(chunks, hand_back)
+            lambda peer: own_out.at[j, peer],
+            lambda own: returned.at[j, :, pl.ds(pl.multiple_of(own * planes, planes), planes)],
+        )
+
+    loop(chunks, own_channel)
 
     def finish(j):
-        await_bytes(arrived4.at[j], recv_sem.at[3, j])
+        await_bytes(returned.at[j], recv_sem.at[3, j])
         for copy in out_copies(j):
             copy.start()
 
@@ -387,12 +370,17 @@
     def close(j):
         for copy in out_copies(j):
             copy.wait()
-        await_bytes(held.at[j, :, pl.ds(0, (planes - 1) * depth)], send_sem.at[0, j])
-        await_bytes(leaving2.at[j, pl.ds(0, depth - 1)], send_sem.at[1, j])
-        await_bytes(leaving3.at[j, pl.ds(0, depth - 1)], send_sem.at[2, j])
-        await_bytes(leaving4.at[j, pl.ds(0, planes - 1)], send_sem.at[3, j])
+        await_bytes(held.at[j, :, pl.ds(0, (depth - 1) * planes)], send_sem.at[0, j])
+        await_bytes(leaving_in.at[j, pl.ds(0, planes - 1)], send_sem.at[1, j])
+        await_bytes(leaving_out.at[j, pl.ds(0, planes - 1)], send_sem.at[2, j])
+        await_bytes(own_out.at[j, pl.ds(0, depth - 1)], send_sem.at[3, j])
 
     loop(chunks, close)
+
+
+def hand_over(filter_in, projected_in, filter_out, projected_out):
+    filter_out[...] = filter_in[...]
+    projected_out[...] = projected_in[...]
 
 
 def on_device(projected, short_taps, long_filter, skip_gain, cotangent):
@@ -403,15 +391,6 @@
     planes = rows * 2
     slots = planes * depth
     chunks = channels // slots
-    col = lax.axis_index("col")
-    place = (lax.axis_index("row") * 2 + col % 2) * depth + col // 2
-    taps = lax.dynamic_slice_in_dim(
-        short_taps.reshape(3, chunks, slots, 3), place, 1, 2
-    ).reshape(3, chunks, 3)
-    gain = lax.dynamic_slice_in_dim(skip_gain.reshape(chunks, slots), place, 1, 1)
-    scalars = jnp.concatenate(
-        [jnp.swapaxes(taps, 0, 1).reshape(chunks, 9), gain], axis=1
-    ).reshape(-1)
     made = [jnp.asarray(t) for t in tables(turns, planes, depth)]
     anywhere = pl.BlockSpec(memory_space=pl.ANY)
 
@@ -424,24 +403,26 @@
             jax.ShapeDtypeStruct((channels, turns), BF16),
             jax.ShapeDtypeStruct((3, channels, turns), BF16),
         ),
-        in_specs=[pl.BlockSpec(memory_space=pltpu.SMEM)] + [anywhere] * 7,
+        in_specs=[anywhere] * 9,
         out_specs=(anywhere, anywhere),
         scratch_shapes=[
             vmem(chunks, 5, slots, turns),
+            vmem(chunks, depth, 5, planes, turns),
             vmem(chunks, planes, 5, depth, turns),
-            vmem(chunks, depth, 5, planes, turns),
-            vmem(chunks, depth, 5, planes, turns),
-            vmem(chunks, depth, 4, planes, turns),
+            vmem(chunks, planes, 5, depth, turns),
             vmem(chunks, depth, 4, planes, turns),
             vmem(chunks, planes, 4, depth, turns),
+            vmem(chunks, planes, 4, depth, turns),
             vmem(chunks, 4, slots, turns),
+            vmem(3, 3, channels, dtype=F32),
+            vmem(1, channels, dtype=F32),
             *[pltpu.VMEM(t.shape, t.dtype) for t in made],
             vmem(slots, turns, dtype=F32),
             vmem(5, slots, turns, dtype=F32),
             vmem(3 * PAD, 2 * slots, dtype=F32),
             vmem(2, 3 * PAD, 2 * slots),
             pltpu.SemaphoreType.DMA((chunks, 3)),
-            pltpu.SemaphoreType.DMA((4,)),
+            pltpu.SemaphoreType.DMA((6,)),
             pltpu.SemaphoreType.DMA((4, chunks)),
             pltpu.SemaphoreType.DMA((4, chunks)),
             pltpu.SemaphoreType.DMA((chunks, 2)),
@@ -450,12 +431,29 @@
             collective_id=0, has_side_effects=True, vmem_limit_bytes=56 << 20
         ),
     )(
-        scalars,
+        jnp.swapaxes(short_taps, 1, 2),
+        skip_gain.reshape(1, channels),
         projected.reshape(3, channels, turns),
         long_filter.reshape(channels, turns),
         cotangent.reshape(channels, turns),
         *made,
     )
+    part = channels // 4
+    blocks = (
+        pl.BlockSpec((part, turns), lambda i: (i, 0)),
+        pl.BlockSpec((3, part, turns), lambda i: (0, i, 0)),
+    )
+    filter_grad, projected_grad = pl.pallas_call(
+        hand_over,
+        out_shape=(
+            jax.ShapeDtypeStruct((channels, turns), BF16),
+            jax.ShapeDtypeStruct((3, channels, turns), BF16),
+        ),
+        grid=(4,),
+        in_specs=blocks,
+        out_specs=blocks,
+        compiler_params=pltpu.CompilerParams(vmem_limit_bytes=56 << 20),
+    )(filter_grad, projected_grad)
     return (
         filter_grad.reshape(channels, 1, 1, turns),
         projected_grad.reshape(3, channels, 1, 1, turns),

time: 255 us -> 230 us (0.902); the launches traced: 251 us -> 230 us
  Pallas kernels: 243 us -> 229 us
  local copies, waits for them, and re-layouts: 7.21 us -> 0 us
    pallas_call x1, Pallas kernels: 243 us -> 225 us  [on_device(): pl.pallas_call(functools.partial(kernel, planes, depth), out_shape=(jax.S...]
    unnamed x2 -> x0, local copies, waits for them, and re-layouts: 4.52 us -> none
    pallas_call x0 -> x1, Pallas kernels: none -> 3.81 us  [on_device(): pl.pallas_call(hand_over, out_shape=(jax.ShapeDtypeStruct((channels, turn...]
where the time goes in v3:
time: 230 us
  Pallas kernels  229 us (100%)
    pallas_call x1, Pallas kernels, on_device(): pl.pallas_call(functools.partial(kernel, planes, depth), out_shape=(jax.S...  225 us

profile of v3, /device:TPU:1, one launch (start us, length us, event | category | flops | bytes accessed | tf_op | source)
XLA Modules:
  0.0 229.9 jit_solution(15732549790321189960)
XLA Ops:
  0.6 225.4 %shard_map.104 = (bf16[2048,128]{1,0:T(8,128)(2,1)}, bf16[3,2048,128]{2,1,0:T(8,128)(2,1)}) custom-call(f32[3,3,2048]{2,1,0:T(4,128)} %bitcast.12, f32[1,2048]{1,0:T(1,128)} %bitcast.13, bf16[3,2048,128]{2,1,0:T(8,128)(2,1)} %bitcast.9, bf16[2048,128]{1,0:T(8,128)(2,1)} %bitcast.10, bf16[2048,128]{1,0:T(8,128)(2,1)} %bitcast.11, ...), custom_call_target="tpu_custom_call" | custom-call | tf_op jit(solution)/shard_map/pallas_call | solution.py:400
  226.1 3.8 %shard_map.105 = (bf16[2048,128]{1,0:T(8,128)(2,1)}, bf16[3,2048,128]{2,1,0:T(8,128)(2,1)}) custom-call(bf16[2048,128]{1,0:T(8,128)(2,1)} %get-tuple-element.6.filter_in, bf16[3,2048,128]{2,1,0:T(8,128)(2,1)} %get-tuple-element.7.projected_in), custom_call_target="tpu_custom_call" | custom-call | tf_op jit(solution)/shard_map/pallas_call | solution.py:446

commit v4 on v3

--- a/solution.py
+++ b/solution.py
@@ -74,7 +74,11 @@
     block_hbm,
     filter_out,
     projected_out,
-    held,
+    raw,
+    raw_near,
+    filter_in,
+    products,
+    kept,
     own_in,
     leaving_in,
     arrived_in,
@@ -82,6 +86,10 @@
     leaving_out,
     arrived_out,
     returned,
+    grads,
+    grads_near,
+    result,
+    columns_of,
     taps,
     gains,
     first,
@@ -89,22 +97,27 @@
     twist,
     block,
     flat,
-    lines,
     spectra,
     factors,
     load_sem,
     table_sem,
     send_sem,
     recv_sem,
+    halo_send,
+    halo_recv,
     out_sem,
 ):
-    chunks = held.shape[0]
-    turns = held.shape[-1]
+    chunks = filter_in.shape[0]
+    turns = filter_in.shape[-1]
     slots = planes * depth
+    half = slots // 2
+    rows_all = planes // 2
     row = lax.axis_index("row")
     col = lax.axis_index("col")
     z = col // 2
-    g = row * 2 + lax.rem(col, 2)
+    y = lax.rem(col, 2)
+    g = row * 2 + y
+    rank = row * 2 * depth + col
 
     def at_plane(step):
         peer = lax.rem(g + step + 1, planes)
@@ -113,7 +126,16 @@
     def at_depth(step):
         away = (1 - 2 * lax.rem(step, 2)) * (step // 2 + 1)
         peer = lax.rem(z + away + depth, depth)
-        return peer, (row, peer * 2 + lax.rem(col, 2))
+        return peer, (row, peer * 2 + y)
+
+    up, down = z + 1, z + depth - 1
+    two_later = (lax.rem(row + up // depth, rows_all), lax.rem(up, depth) * 2 + y)
+    two_earlier = (
+        lax.rem(row + rows_all - 1 + down // depth, rows_all),
+        lax.rem(down, depth) * 2 + y,
+    )
+    partner = (row, z * 2 + 1 - y)
+    sides = (pl.ds(0, half), pl.ds(half, half))
 
     def await_bytes(ref, sem):
         pltpu.make_async_copy(ref, ref, sem).wait()
@@ -122,10 +144,10 @@
         rows = pl.ds(j * slots, slots)
         return (
             pltpu.make_async_copy(
-                projected.at[:, rows], held.at[j, pl.ds(0, 3)], load_sem.at[j, 0]
+                projected.at[:, rows], raw.at[j, 0, pl.ds(0, 3)], load_sem.at[j, 0]
             ),
-            pltpu.make_async_copy(filt.at[rows], held.at[j, 3], load_sem.at[j, 1]),
-            pltpu.make_async_copy(cotangent.at[rows], held.at[j, 4], load_sem.at[j, 2]),
+            pltpu.make_async_copy(cotangent.at[rows], raw.at[j, 0, 3], load_sem.at[j, 1]),
+            pltpu.make_async_copy(filt.at[rows], filter_in.at[j], load_sem.at[j, 2]),
         )
 
     def table_copies():
@@ -145,10 +167,40 @@
     def out_copies(j):
         rows = pl.ds(j * slots, slots)
         return (
-            pltpu.make_async_copy(
-                returned.at[j, pl.ds(0, 3)], projected_out.at[:, rows], out_sem.at[j, 0]
-            ),
-            pltpu.make_async_copy(returned.at[j, 3], filter_out.at[rows], out_sem.at[j, 1]),
+            pltpu.make_async_copy(result.at[j], projected_out.at[:, rows], out_sem.at[j, 0]),
+            pltpu.make_async_copy(returned.at[j, 2], filter_out.at[rows], out_sem.at[j, 1]),
+        )
+
+    def halo(kind, j, source, target, device):
+        return pltpu.make_async_remote_copy(
+            src_ref=source,
+            dst_ref=target,
+            send_sem=halo_send.at[kind, j],
+            recv_sem=halo_recv.at[kind, j],
+            device_id=device,
+            device_id_type=MESH,
+        )
+
+    def far_halo(way, side, j):
+        arrays = pl.ds(0, 4 if (way, side) == (0, 1) else 3)
+        held = (raw, grads)[way]
+        return halo(
+            way * 2 + side,
+            j,
+            held.at[j, 0, arrays, sides[side]],
+            held.at[j, 1, arrays, sides[side]],
+            two_later if way == side else two_earlier,
+        )
+
+    def near_halo(way, side, j):
+        held, near = ((raw, raw_near), (grads, grads_near))[way]
+        own_or_far = y if way == side else 1 - y
+        return halo(
+            4 + way * 2 + side,
+            j,
+            held.at[j, own_or_far, pl.ds(0, 3), sides[side]],
+            near.at[j, :, sides[side]],
+            partner,
         )
 
     def loop(count, body):
@@ -171,10 +223,12 @@
 
     loop(depth - 1, greet(at_depth))
     loop(planes - 1, greet(at_plane))
-    pl.semaphore_wait(barrier, planes + depth - 2)
+    for device in (two_later, two_earlier):
+        pl.semaphore_signal(barrier, inc=1, device_id=device, device_id_type=MESH)
+    pl.semaphore_wait(barrier, planes + depth)
 
     def send_all(phase, j, source, target):
-        count, at, own = (depth, at_depth, z) if phase in (0, 3) else (planes, at_plane, g)
+        count, at, own = (planes, at_plane, g) if phase in (2, 3) else (depth, at_depth, z)
         pltpu.make_async_copy(source(own), target(own), recv_sem.at[phase, j]).start()
 
         def one(i):
@@ -200,38 +254,116 @@
 
         loop(arrays, one)
 
+    def part(peer):
+        return pl.ds(pl.multiple_of(peer * planes, planes), planes)
+
     def enter(j):
         for copy in load_copies(j):
             copy.wait()
-        send_all(
-            0,
-            j,
-            lambda peer: held.at[j, :, pl.ds(pl.multiple_of(peer * planes, planes), planes)],
-            lambda own: own_in.at[j, own],
-        )
+        for side in range(2):
+            far_halo(0, side, j).start()
+        send_all(0, j, lambda peer: filter_in.at[j, part(peer)], lambda own: own_in.at[j, own, 0])
 
     loop(chunks, enter)
     for copy in table_copies():
         copy.wait()
 
-    row_of = lax.broadcasted_iota(jnp.int32, (slots, turns), 0)
-    odd = lax.rem(row_of, 2) == 1
-    edge_row = lax.broadcasted_iota(jnp.int32, (planes, turns), 0)
-    edge_lane = lax.broadcasted_iota(jnp.int32, (planes, turns), 1)
-
-    def earlier(now):
-        edge = pltpu.roll(now[slots - planes :], 2, 0)
-        wrapped = jnp.where(edge_lane == 0, 0.0, pltpu.roll(edge, 1, 1))
-        edge = jnp.where(edge_row < 2, wrapped, edge)
-        second = jnp.concatenate([edge, now[: slots - planes]], axis=0)
-        return jnp.where(odd, pltpu.roll(now, 1, 0), pltpu.roll(second, slots - 1, 0)), second
-
-    def later(now):
-        edge = pltpu.roll(now[:planes], planes - 2, 0)
-        wrapped = jnp.where(edge_lane == turns - 1, 0.0, pltpu.roll(edge, turns - 1, 1))
-        edge = jnp.where(edge_row >= planes - 2, wrapped, edge)
-        second = jnp.concatenate([now[planes:], edge], axis=0)
-        return jnp.where(odd, pltpu.roll(second, 1, 0), pltpu.roll(now, slots - 1, 0)), second
+    def make_columns(j):
+        mine = pl.ds(pl.multiple_of(j * slots, slots), slots)
+        which = lax.broadcasted_iota(jnp.int32, (16, slots), 0)
+        packed = jnp.where(which == 9, gains[:, mine], 0.0)
+        for i in range(3):
+            for t in range(3):
+                packed = jnp.where(which == i * 3 + t, taps[i, pl.ds(t, 1), mine], packed)
+        columns_of[j] = jnp.transpose(packed)
+
+    loop(chunks, make_columns)
+
+    lane = lax.broadcasted_iota(jnp.int32, (half, turns), 1)
+    ranks = jnp.full((half, turns), rank, jnp.int32)
+    final = lane == turns - 1
+    last_two, last_one, next_last = ranks >= slots - 2, ranks == slots - 1, ranks == slots - 2
+    first_two, first_one = ranks < 2, ranks == 0
+
+    def wrap_back(values, where, fill):
+        moved = pltpu.roll(values, 1, 1)
+        if fill:
+            moved = jnp.where(lane == 0, 0.0, moved)
+        return jnp.where(where, moved, values)
+
+    def wrap_ahead(values, where, fill):
+        moved = pltpu.roll(values, turns - 1, 1)
+        if fill:
+            moved = jnp.where(final, 0.0, moved)
+        return jnp.where(where, moved, values)
+
+    def drop(values, where):
+        return jnp.where(jnp.logical_and(final, where), 0.0, values)
+
+    def column(j, side, k):
+        return columns_of[j, sides[side], pl.ds(k, 1)]
+
+    def filtered(j, side, i, lines):
+        return (
+            column(j, side, i * 3) * lines[0]
+            + column(j, side, i * 3 + 1) * lines[1]
+            + column(j, side, i * 3 + 2) * lines[2]
+        )
+
+    def pass_near(way):
+        def one(j):
+            for side in range(2):
+                far_halo(way, side, j).wait_recv()
+                near_halo(way, side, j).start()
+
+        return one
+
+    def make_products(j):
+        for side in range(2):
+            rows = sides[side]
+            near_halo(0, side, j).wait_recv()
+
+            def feature(i):
+                own = raw[j, 0, i, rows].astype(F32)
+                near = raw_near[j, i, rows].astype(F32)
+                far = raw[j, 1, i, rows].astype(F32)
+                if side == 0:
+                    near = wrap_back(near, first_one, True)
+                    far = wrap_back(far, first_two, True)
+                    return filtered(j, side, i, (own, near, far))
+                far = wrap_ahead(far, last_two, False)
+                near = drop(wrap_ahead(near, last_one, False), next_last)
+                return filtered(j, side, i, (far, near, drop(own, last_two)))
+
+            if side == 0:
+                seed = raw[j, 0, 3, rows].astype(F32)
+            else:
+                seed = wrap_ahead(raw[j, 1, 3, rows].astype(F32), last_two, False)
+            kept[j, 3, rows] = seed
+            weighted = feature(0) * seed
+            kept[j, 2, rows] = weighted
+            products[j, 1, rows] = weighted.astype(BF16)
+            keys = feature(1)
+            kept[j, 0, rows] = keys
+            values = feature(2)
+            kept[j, 1, rows] = values
+            products[j, 0, rows] = (keys * values).astype(BF16)
+        send_all(
+            1,
+            j,
+            lambda peer: products.at[j, :, part(peer)],
+            lambda own: own_in.at[j, own, pl.ds(1, 2)],
+        )
+
+    def products_in_turn(j):
+        @pl.when(j + 1 < chunks)
+        def _():
+            pass_near(0)(j + 1)
+
+        make_products(j)
+
+    pass_near(0)(0)
+    loop(chunks, products_in_turn)
 
     def transform():
         width = min(256, 2 * slots)
@@ -257,57 +389,29 @@
         return spectra[rows, pl.ds(0, slots)], spectra[rows, pl.ds(slots, slots)]
 
     def own_channel(j):
-        await_bytes(own_in.at[j], recv_sem.at[0, j])
+        await_bytes(own_in.at[j, :, 0], recv_sem.at[0, j])
+        await_bytes(own_in.at[j, :, pl.ds(1, 2)], recv_sem.at[1, j])
         exchange(own_in, leaving_in, j)
-        send_all(1, j, lambda peer: leaving_in.at[j, peer], lambda own: arrived_in.at[j, own])
-        await_bytes(arrived_in.at[j], recv_sem.at[1, j])
+        send_all(2, j, lambda peer: leaving_in.at[j, peer], lambda own: arrived_in.at[j, own])
+        await_bytes(arrived_in.at[j], recv_sem.at[2, j])
         exchange(arrived_in, own_in, j)
 
-        mine = pl.ds(pl.multiple_of(j * slots, slots), slots)
-        here = lax.broadcasted_iota(jnp.int32, (1, slots), 1) == z * planes + g
-
-        def pick(values):
-            return jnp.sum(jnp.where(here, values, 0.0), axis=1, keepdims=True)
-
-        tap = [[pick(taps[i, pl.ds(t, 1), mine]) for t in range(3)] for i in range(3)]
-        gain = pick(gains[:, mine])
-
-        def line(i):
-            return own_in[j, :, i].astype(F32).reshape(slots, turns)
-
-        def feature(i):
-            now = line(i)
-            first_back, second_back = earlier(now)
-            return (
-                tap[i][0] * now
-                + tap[i][1] * first_back
-                + tap[i][2] * second_back
-            )
-
-        lines[0] = feature(1)
-        lines[1] = feature(2)
-        lines[2] = lines[0] * lines[1]
-        lines[3] = line(3)
-        lines[4] = feature(0) * line(4)
-
         def spectrum(i):
-            high, low = split(lines[2 + i])
-            turned = dot_t(first[0], high) + (dot_t(first[0], low) + dot_t(first[1], high))
+            line = own_in[j, :, i].reshape(slots, turns)
+            turned = dot_t(first[0], line) + dot_t(first[1], line)
             real, imag = turned[:PAD], turned[PAD:]
             put(i, real * twist[0] + imag * twist[1], imag * twist[0] - real * twist[1])
 
         for i in range(3):
             spectrum(i)
         transform()
-        gated_re, gated_im = get(0)
-        filt_re, filt_im = get(1)
+        filt_re, filt_im = get(0)
+        gated_re, gated_im = get(1)
         put(
             0,
             gated_re * filt_re - gated_im * filt_im,
             -(gated_re * filt_im) - gated_im * filt_re,
         )
-        gated_re, gated_im = get(0)
-        filt_re, filt_im = get(1)
         side_re, side_im = get(2)
         put(
             1,
@@ -327,53 +431,72 @@
                 [real * twist[0] + imag * twist[1], imag * twist[0] - real * twist[1]], axis=0
             )
             high, low = split(turned)
-            result = dot(last[0], high) + (dot(last[0], low) + dot(last[1], high))
-            return jnp.transpose(result)
-
-        lines[2] = back(0) + gain * lines[2]
-        lines[4] = back(1) + gain * lines[4]
-        own_out[j, :, 3] = back(2).astype(BF16).reshape(depth, planes, turns)
-
-        def leave(i, grad):
-            now = grad.astype(BF16).astype(F32)
-            first_next, second_next = later(now)
-            total = (
-                tap[i][0] * now
-                + tap[i][1] * first_next
-                + tap[i][2] * second_next
-            )
-            own_out[j, :, i] = total.astype(BF16).reshape(depth, planes, turns)
-
-        leave(0, line(4) * lines[2])
-        leave(1, lines[4] * lines[1])
-        leave(2, lines[4] * lines[0])
+            line = dot(last[0], high) + (dot(last[0], low) + dot(last[1], high))
+            own_out[j, :, i] = jnp.transpose(line).astype(BF16).reshape(depth, planes, turns)
+
+        for i in range(3):
+            back(i)
         exchange(own_out, leaving_out, j)
-        send_all(2, j, lambda peer: leaving_out.at[j, peer], lambda own: arrived_out.at[j, own])
-        await_bytes(arrived_out.at[j], recv_sem.at[2, j])
+        send_all(3, j, lambda peer: leaving_out.at[j, peer], lambda own: arrived_out.at[j, own])
+        await_bytes(arrived_out.at[j], recv_sem.at[3, j])
         exchange(arrived_out, own_out, j)
         send_all(
-            3,
-            j,
-            lambda peer: own_out.at[j, peer],
-            lambda own: returned.at[j, :, pl.ds(pl.multiple_of(own * planes, planes), planes)],
+            4, j, lambda peer: own_out.at[j, peer], lambda own: returned.at[j, :, part(own)]
         )
 
     loop(chunks, own_channel)
 
+    def make_grads(j):
+        await_bytes(returned.at[j], recv_sem.at[4, j])
+        out_copies(j)[1].start()
+        for side in range(2):
+            rows = sides[side]
+            gain = column(j, side, 9)
+            keys, values = kept[j, 0, rows], kept[j, 1, rows]
+            mixed = returned[j, 0, rows].astype(F32) + gain * (keys * values)
+            grads[j, 0, 0, rows] = (kept[j, 3, rows] * mixed).astype(BF16)
+            gated_grad = returned[j, 1, rows].astype(F32) + gain * kept[j, 2, rows]
+            grads[j, 0, 1, rows] = (gated_grad * values).astype(BF16)
+            grads[j, 0, 2, rows] = (gated_grad * keys).astype(BF16)
+            far_halo(1, side, j).start()
+
+    loop(chunks, make_grads)
+    loop(chunks, pass_near(1))
+
     def finish(j):
-        await_bytes(returned.at[j], recv_sem.at[3, j])
-        for copy in out_copies(j):
-            copy.start()
+        for side in range(2):
+            rows = sides[side]
+            near_halo(1, side, j).wait_recv()
+            for i in range(3):
+                own = grads[j, 0, i, rows].astype(F32)
+                near = grads_near[j, i, rows].astype(F32)
+                far = grads[j, 1, i, rows].astype(F32)
+                if side == 0:
+                    near = wrap_ahead(near, last_one, True)
+                    far = wrap_ahead(far, last_two, True)
+                    total = filtered(j, side, i, (own, near, far))
+                else:
+                    far = wrap_back(far, first_two, False)
+                    near = drop(wrap_back(near, first_one, False), last_one)
+                    total = filtered(j, side, i, (far, near, drop(own, last_two)))
+                result[j, i, rows] = total.astype(BF16)
+        out_copies(j)[0].start()
 
     loop(chunks, finish)
 
     def close(j):
         for copy in out_copies(j):
             copy.wait()
-        await_bytes(held.at[j, :, pl.ds(0, (depth - 1) * planes)], send_sem.at[0, j])
-        await_bytes(leaving_in.at[j, pl.ds(0, planes - 1)], send_sem.at[1, j])
-        await_bytes(leaving_out.at[j, pl.ds(0, planes - 1)], send_sem.at[2, j])
-        await_bytes(own_out.at[j, pl.ds(0, depth - 1)], send_sem.at[3, j])
+        others = pl.ds(0, (depth - 1) * planes)
+        await_bytes(filter_in.at[j, others], send_sem.at[0, j])
+        await_bytes(products.at[j, :, others], send_sem.at[1, j])
+        await_bytes(leaving_in.at[j, pl.ds(0, planes - 1)], send_sem.at[2, j])
+        await_bytes(leaving_out.at[j, pl.ds(0, planes - 1)], send_sem.at[3, j])
+        await_bytes(own_out.at[j, pl.ds(0, depth - 1)], send_sem.at[4, j])
+        for way in range(2):
+            for side in range(2):
+                far_halo(way, side, j).wait_send()
+                near_halo(way, side, j).wait_send()
 
     loop(chunks, close)
 
@@ -406,25 +529,34 @@
         in_specs=[anywhere] * 9,
         out_specs=(anywhere, anywhere),
         scratch_shapes=[
-            vmem(chunks, 5, slots, turns),
-            vmem(chunks, depth, 5, planes, turns),
-            vmem(chunks, planes, 5, depth, turns),
-            vmem(chunks, planes, 5, depth, turns),
-            vmem(chunks, depth, 4, planes, turns),
-            vmem(chunks, planes, 4, depth, turns),
-            vmem(chunks, planes, 4, depth, turns),
-            vmem(chunks, 4, slots, turns),
+            vmem(chunks, 2, 4, slots, turns),
+            vmem(chunks, 3, slots, turns),
+            vmem(chunks, slots, turns),
+            vmem(chunks, 2, slots, turns),
+            vmem(chunks, 4, slots, turns, dtype=F32),
+            vmem(chunks, depth, 3, planes, turns),
+            vmem(chunks, planes, 3, depth, turns),
+            vmem(chunks, planes, 3, depth, turns),
+            vmem(chunks, depth, 3, planes, turns),
+            vmem(chunks, planes, 3, depth, turns),
+            vmem(chunks, planes, 3, depth, turns),
+            vmem(chunks, 3, slots, turns),
+            vmem(chunks, 2, 3, slots, turns),
+            vmem(chunks, 3, slots, turns),
+            vmem(chunks, 3, slots, turns),
+            vmem(chunks, slots, 16, dtype=F32),
             vmem(3, 3, channels, dtype=F32),
             vmem(1, channels, dtype=F32),
             *[pltpu.VMEM(t.shape, t.dtype) for t in made],
             vmem(slots, turns, dtype=F32),
-            vmem(5, slots, turns, dtype=F32),
             vmem(3 * PAD, 2 * slots, dtype=F32),
             vmem(2, 3 * PAD, 2 * slots),
             pltpu.SemaphoreType.DMA((chunks, 3)),
             pltpu.SemaphoreType.DMA((6,)),
-            pltpu.SemaphoreType.DMA((4, chunks)),
-            pltpu.SemaphoreType.DMA((4, chunks)),
+            pltpu.SemaphoreType.DMA((5, chunks)),
+            pltpu.SemaphoreType.DMA((5, chunks)),
+            pltpu.SemaphoreType.DMA((8, chunks)),
+            pltpu.SemaphoreType.DMA((8, chunks)),
             pltpu.SemaphoreType.DMA((chunks, 2)),
         ],
         compiler_params=pltpu.CompilerParams(

time: 230 us -> 246 us (1.070)
  Pallas kernels: 229 us -> 245 us
    pallas_call x1, Pallas kernels: 225 us -> 241 us  [on_device(): pl.pallas_call(functools.partial(kernel, planes, depth), out_shape=(jax.S...]
where the time goes in v4:
time: 246 us
  Pallas kernels  245 us (100%)
    pallas_call x1, Pallas kernels, on_device(): pl.pallas_call(functools.partial(kernel, planes, depth), out_shape=(jax.S...  241 us

profile of v4, /device:TPU:1, one launch (start us, length us, event | category | flops | bytes accessed | tf_op | source)
XLA Modules:
  0.0 245.8 jit_solution(17181805584142423343)
XLA Ops:
  0.6 241.3 %shard_map.104 = (bf16[2048,128]{1,0:T(8,128)(2,1)}, bf16[3,2048,128]{2,1,0:T(8,128)(2,1)}) custom-call(f32[3,3,2048]{2,1,0:T(4,128)} %bitcast.12, f32[1,2048]{1,0:T(1,128)} %bitcast.13, bf16[3,2048,128]{2,1,0:T(8,128)(2,1)} %bitcast.9, bf16[2048,128]{1,0:T(8,128)(2,1)} %bitcast.10, bf16[2048,128]{1,0:T(8,128)(2,1)} %bitcast.11, ...), custom_call_target="tpu_custom_call" | custom-call | tf_op jit(solution)/shard_map/pallas_call | solution.py:523
  242.0 3.8 %shard_map.105 = (bf16[2048,128]{1,0:T(8,128)(2,1)}, bf16[3,2048,128]{2,1,0:T(8,128)(2,1)}) custom-call(bf16[2048,128]{1,0:T(8,128)(2,1)} %get-tuple-element.6.filter_in, bf16[3,2048,128]{2,1,0:T(8,128)(2,1)} %get-tuple-element.7.projected_in), custom_call_target="tpu_custom_call" | custom-call | tf_op jit(solution)/shard_map/pallas_call | solution.py:578

commit v5 on v4

--- a/solution.py
+++ b/solution.py
@@ -90,6 +90,15 @@
     grads_near,
     result,
     columns_of,
+    whole_held,
+    whole_in,
+    whole_leaving_in,
+    whole_arrived_in,
+    whole_out,
+    whole_leaving_out,
+    whole_arrived_out,
+    whole_returned,
+    lines,
     taps,
     gains,
     first,
@@ -140,6 +149,34 @@
     def await_bytes(ref, sem):
         pltpu.make_async_copy(ref, ref, sem).wait()
 
+    early, middle = depth // 2, depth * 5 // 8
+    whole = chunks * slots
+
+    def load_whole():
+        rows = pl.ds(whole, slots)
+        return (
+            pltpu.make_async_copy(
+                projected.at[:, rows], whole_held.at[0, pl.ds(0, 3)], load_sem.at[chunks, 0]
+            ),
+            pltpu.make_async_copy(filt.at[rows], whole_held.at[0, 3], load_sem.at[chunks, 1]),
+            pltpu.make_async_copy(
+                cotangent.at[rows], whole_held.at[0, 4], load_sem.at[chunks, 2]
+            ),
+        )
+
+    def whole_copies():
+        rows = pl.ds(whole, slots)
+        return (
+            pltpu.make_async_copy(
+                whole_returned.at[0, pl.ds(0, 3)],
+                projected_out.at[:, rows],
+                out_sem.at[chunks, 0],
+            ),
+            pltpu.make_async_copy(
+                whole_returned.at[0, 3], filter_out.at[rows], out_sem.at[chunks, 1]
+            ),
+        )
+
     def load_copies(j):
         rows = pl.ds(j * slots, slots)
         return (
@@ -209,6 +246,8 @@
     for j in range(chunks):
         for copy in load_copies(j):
             copy.start()
+    for copy in load_whole():
+        copy.start()
     for copy in table_copies():
         copy.start()
 
@@ -227,9 +266,11 @@
         pl.semaphore_signal(barrier, inc=1, device_id=device, device_id_type=MESH)
     pl.semaphore_wait(barrier, planes + depth)
 
-    def send_all(phase, j, source, target):
-        count, at, own = (planes, at_plane, g) if phase in (2, 3) else (depth, at_depth, z)
-        pltpu.make_async_copy(source(own), target(own), recv_sem.at[phase, j]).start()
+    def send_all(phase, j, source, target, start=0, stop=None):
+        count, at, own = (planes, at_plane, g) if phase in (2, 3, 6, 7) else (depth, at_depth, z)
+        stop = count - 1 if stop is None else stop
+        if start == 0:
+            pltpu.make_async_copy(source(own), target(own), recv_sem.at[phase, j]).start()
 
         def one(i):
             peer, device = at(i)
@@ -242,7 +283,7 @@
                 device_id_type=MESH,
             ).start()
 
-        loop(count - 1, one)
+        lax.fori_loop(start, stop, lambda i, carry: (one(i), carry)[1], 0)
 
     def exchange(source, target, j):
         outer, arrays, inner = source.shape[1:4]
@@ -265,6 +306,8 @@
         send_all(0, j, lambda peer: filter_in.at[j, part(peer)], lambda own: own_in.at[j, own, 0])
 
     loop(chunks, enter)
+    for copy in load_whole():
+        copy.wait()
     for copy in table_copies():
         copy.wait()
 
@@ -364,6 +407,12 @@
 
     pass_near(0)(0)
     loop(chunks, products_in_turn)
+    send_all(
+        5,
+        0,
+        lambda peer: whole_held.at[0, :, part(peer)],
+        lambda own: whole_in.at[0, own],
+    )
 
     def transform():
         width = min(256, 2 * slots)
@@ -388,22 +437,30 @@
         rows = pl.ds(i * PAD, PAD)
         return spectra[rows, pl.ds(0, slots)], spectra[rows, pl.ds(slots, slots)]
 
-    def own_channel(j):
-        await_bytes(own_in.at[j, :, 0], recv_sem.at[0, j])
-        await_bytes(own_in.at[j, :, pl.ds(1, 2)], recv_sem.at[1, j])
-        exchange(own_in, leaving_in, j)
-        send_all(2, j, lambda peer: leaving_in.at[j, peer], lambda own: arrived_in.at[j, own])
-        await_bytes(arrived_in.at[j], recv_sem.at[2, j])
-        exchange(arrived_in, own_in, j)
-
-        def spectrum(i):
-            line = own_in[j, :, i].reshape(slots, turns)
-            turned = dot_t(first[0], line) + dot_t(first[1], line)
+    row_of = lax.broadcasted_iota(jnp.int32, (slots, turns), 0)
+    odd = lax.rem(row_of, 2) == 1
+    edge_row = lax.broadcasted_iota(jnp.int32, (planes, turns), 0)
+    edge_lane = lax.broadcasted_iota(jnp.int32, (planes, turns), 1)
+
+    def earlier(now):
+        edge = pltpu.roll(now[slots - planes :], 2, 0)
+        wrapped = jnp.where(edge_lane == 0, 0.0, pltpu.roll(edge, 1, 1))
+        edge = jnp.where(edge_row < 2, wrapped, edge)
+        second = jnp.concatenate([edge, now[: slots - planes]], axis=0)
+        return jnp.where(odd, pltpu.roll(now, 1, 0), pltpu.roll(second, slots - 1, 0)), second
+
+    def later(now):
+        edge = pltpu.roll(now[:planes], planes - 2, 0)
+        wrapped = jnp.where(edge_lane == turns - 1, 0.0, pltpu.roll(edge, turns - 1, 1))
+        edge = jnp.where(edge_row >= planes - 2, wrapped, edge)
+        second = jnp.concatenate([now[planes:], edge], axis=0)
+        return jnp.where(odd, pltpu.roll(second, 1, 0), pltpu.roll(now, slots - 1, 0)), second
+
+    def spectral(analyse, keep):
+        for i in range(3):
+            turned = analyse(i)
             real, imag = turned[:PAD], turned[PAD:]
             put(i, real * twist[0] + imag * twist[1], imag * twist[0] - real * twist[1])
-
-        for i in range(3):
-            spectrum(i)
         transform()
         filt_re, filt_im = get(0)
         gated_re, gated_im = get(1)
@@ -425,26 +482,140 @@
         )
         transform()
 
-        def back(i):
+        for i in range(3):
             real, imag = get(i)
             turned = jnp.concatenate(
                 [real * twist[0] + imag * twist[1], imag * twist[0] - real * twist[1]], axis=0
             )
             high, low = split(turned)
             line = dot(last[0], high) + (dot(last[0], low) + dot(last[1], high))
-            own_out[j, :, i] = jnp.transpose(line).astype(BF16).reshape(depth, planes, turns)
-
-        for i in range(3):
-            back(i)
+            keep(i, jnp.transpose(line))
+
+    def whole_gather():
+        await_bytes(whole_in.at[0], recv_sem.at[5, 0])
+        exchange(whole_in, whole_leaving_in, 0)
+        send_all(
+            6,
+            0,
+            lambda peer: whole_leaving_in.at[0, peer],
+            lambda own: whole_arrived_in.at[0, own],
+        )
+
+    def whole_channel():
+        await_bytes(whole_arrived_in.at[0], recv_sem.at[6, 0])
+        exchange(whole_arrived_in, whole_in, 0)
+        mine = pl.ds(whole, slots)
+        here = lax.broadcasted_iota(jnp.int32, (1, slots), 1) == z * planes + g
+
+        def pick(values):
+            return jnp.sum(jnp.where(here, values, 0.0), axis=1, keepdims=True)
+
+        tap = [[pick(taps[i, pl.ds(t, 1), mine]) for t in range(3)] for i in range(3)]
+        gain = pick(gains[:, mine])
+
+        def line(i):
+            return whole_in[0, :, i].astype(F32).reshape(slots, turns)
+
+        def feature(i):
+            now = line(i)
+            first_back, second_back = earlier(now)
+            return tap[i][0] * now + tap[i][1] * first_back + tap[i][2] * second_back
+
+        lines[0] = line(3)
+        lines[3] = feature(1)
+        lines[4] = feature(2)
+        lines[1] = lines[3] * lines[4]
+        lines[2] = feature(0) * line(4)
+
+        def analyse(i):
+            high, low = split(lines[i])
+            return dot_t(first[0], high) + (dot_t(first[0], low) + dot_t(first[1], high))
+
+        def keep(i, result_line):
+            if i == 2:
+                whole_out[0, :, 3] = result_line.astype(BF16).reshape(depth, planes, turns)
+            else:
+                lines[1 + i] = result_line + gain * lines[1 + i]
+
+        spectral(analyse, keep)
+
+        def leave(i, grad):
+            now = grad.astype(BF16).astype(F32)
+            first_next, second_next = later(now)
+            total = tap[i][0] * now + tap[i][1] * first_next + tap[i][2] * second_next
+            whole_out[0, :, i] = total.astype(BF16).reshape(depth, planes, turns)
+
+        leave(0, line(4) * lines[1])
+        leave(1, lines[2] * lines[4])
+        leave(2, lines[2] * lines[3])
+        exchange(whole_out, whole_leaving_out, 0)
+        send_all(
+            7,
+            0,
+            lambda peer: whole_leaving_out.at[0, peer],
+            lambda own: whole_arrived_out.at[0, own],
+        )
+
+    def whole_scatter():
+        await_bytes(whole_arrived_out.at[0], recv_sem.at[7, 0])
+        exchange(whole_arrived_out, whole_out, 0)
+
+    def whole_back(start, stop):
+        send_all(
+            8,
+            0,
+            lambda peer: whole_out.at[0, peer],
+            lambda own: whole_returned.at[0, :, part(own)],
+            start,
+            stop,
+        )
+
+    def gather(j):
+        await_bytes(own_in.at[j, :, 0], recv_sem.at[0, j])
+        await_bytes(own_in.at[j, :, pl.ds(1, 2)], recv_sem.at[1, j])
+        exchange(own_in, leaving_in, j)
+        send_all(2, j, lambda peer: leaving_in.at[j, peer], lambda own: arrived_in.at[j, own])
+
+    def own_channel(j):
+        await_bytes(arrived_in.at[j], recv_sem.at[2, j])
+        exchange(arrived_in, own_in, j)
+
+        def analyse(i):
+            line = own_in[j, :, i].reshape(slots, turns)
+            return dot_t(first[0], line) + dot_t(first[1], line)
+
+        def keep(i, line):
+            own_out[j, :, i] = line.astype(BF16).reshape(depth, planes, turns)
+
+        spectral(analyse, keep)
         exchange(own_out, leaving_out, j)
         send_all(3, j, lambda peer: leaving_out.at[j, peer], lambda own: arrived_out.at[j, own])
+
+    def scatter(j):
         await_bytes(arrived_out.at[j], recv_sem.at[3, j])
         exchange(arrived_out, own_out, j)
         send_all(
             4, j, lambda peer: own_out.at[j, peer], lambda own: returned.at[j, :, part(own)]
         )
 
-    loop(chunks, own_channel)
+    def channel_in_turn(j):
+        own_channel(j)
+
+        @pl.when(j + 1 < chunks)
+        def _():
+            gather(j + 1)
+
+        @pl.when(j + 1 == chunks)
+        def _():
+            whole_gather()
+
+        scatter(j)
+
+    gather(0)
+    loop(chunks, channel_in_turn)
+    whole_channel()
+    whole_scatter()
+    whole_back(0, early)
 
     def make_grads(j):
         await_bytes(returned.at[j], recv_sem.at[4, j])
@@ -460,7 +631,10 @@
             grads[j, 0, 2, rows] = (gated_grad * keys).astype(BF16)
             far_halo(1, side, j).start()
 
-    loop(chunks, make_grads)
+    loop(chunks - 1, make_grads)
+    whole_back(early, middle)
+    make_grads(chunks - 1)
+    whole_back(middle, depth - 1)
     loop(chunks, pass_near(1))
 
     def finish(j):
@@ -483,6 +657,9 @@
         out_copies(j)[0].start()
 
     loop(chunks, finish)
+    await_bytes(whole_returned.at[0], recv_sem.at[8, 0])
+    for copy in whole_copies():
+        copy.start()
 
     def close(j):
         for copy in out_copies(j):
@@ -499,6 +676,12 @@
                 near_halo(way, side, j).wait_send()
 
     loop(chunks, close)
+    for copy in whole_copies():
+        copy.wait()
+    await_bytes(whole_held.at[0, :, pl.ds(0, (depth - 1) * planes)], send_sem.at[5, 0])
+    await_bytes(whole_leaving_in.at[0, pl.ds(0, planes - 1)], send_sem.at[6, 0])
+    await_bytes(whole_leaving_out.at[0, pl.ds(0, planes - 1)], send_sem.at[7, 0])
+    await_bytes(whole_out.at[0, pl.ds(0, depth - 1)], send_sem.at[8, 0])
 
 
 def hand_over(filter_in, projected_in, filter_out, projected_out):
@@ -513,7 +696,7 @@
     depth = lax.axis_size("col") // 2
     planes = rows * 2
     slots = planes * depth
-    chunks = channels // slots
+    chunks = channels // slots - 1
     made = [jnp.asarray(t) for t in tables(turns, planes, depth)]
     anywhere = pl.BlockSpec(memory_space=pl.ANY)
 
@@ -545,19 +728,28 @@
             vmem(chunks, 3, slots, turns),
             vmem(chunks, 3, slots, turns),
             vmem(chunks, slots, 16, dtype=F32),
+            vmem(1, 5, slots, turns),
+            vmem(1, depth, 5, planes, turns),
+            vmem(1, planes, 5, depth, turns),
+            vmem(1, planes, 5, depth, turns),
+            vmem(1, depth, 4, planes, turns),
+            vmem(1, planes, 4, depth, turns),
+            vmem(1, planes, 4, depth, turns),
+            vmem(1, 4, slots, turns),
+            vmem(5, slots, turns, dtype=F32),
             vmem(3, 3, channels, dtype=F32),
             vmem(1, channels, dtype=F32),
             *[pltpu.VMEM(t.shape, t.dtype) for t in made],
             vmem(slots, turns, dtype=F32),
             vmem(3 * PAD, 2 * slots, dtype=F32),
             vmem(2, 3 * PAD, 2 * slots),
-            pltpu.SemaphoreType.DMA((chunks, 3)),
+            pltpu.SemaphoreType.DMA((chunks + 1, 3)),
             pltpu.SemaphoreType.DMA((6,)),
-            pltpu.SemaphoreType.DMA((5, chunks)),
-            pltpu.SemaphoreType.DMA((5, chunks)),
+            pltpu.SemaphoreType.DMA((9, chunks)),
+            pltpu.SemaphoreType.DMA((9, chunks)),
             pltpu.SemaphoreType.DMA((8, chunks)),
             pltpu.SemaphoreType.DMA((8, chunks)),
-            pltpu.SemaphoreType.DMA((chunks, 2)),
+            pltpu.SemaphoreType.DMA((chunks + 1, 2)),
         ],
         compiler_params=pltpu.CompilerParams(
             collective_id=0, has_side_effects=True, vmem_limit_bytes=56 << 20

time: 246 us -> 211 us (0.86)
  Pallas kernels: 245 us -> 210 us
    pallas_call x1, Pallas kernels: 241 us -> 206 us  [on_device(): pl.pallas_call(functools.partial(kernel, planes, depth), out_shape=(jax.S...]
where the time goes in v5:
time: 211 us; the launch traced here: 210 us
  Pallas kernels  210 us (100%)
    pallas_call x1, Pallas kernels, on_device(): pl.pallas_call(functools.partial(kernel, planes, depth), out_shape=(jax.S...  206 us

profile of v5, /device:TPU:1, one launch (start us, length us, event | category | flops | bytes accessed | tf_op | source)
XLA Modules:
  0.0 210.2 jit_solution(3092613074667071818)
XLA Ops:
  0.6 205.8 %shard_map.104 = (bf16[2048,128]{1,0:T(8,128)(2,1)}, bf16[3,2048,128]{2,1,0:T(8,128)(2,1)}) custom-call(f32[3,3,2048]{2,1,0:T(4,128)} %bitcast.12, f32[1,2048]{1,0:T(1,128)} %bitcast.13, bf16[3,2048,128]{2,1,0:T(8,128)(2,1)} %bitcast.9, bf16[2048,128]{1,0:T(8,128)(2,1)} %bitcast.10, bf16[2048,128]{1,0:T(8,128)(2,1)} %bitcast.11, ...), custom_call_target="tpu_custom_call" | custom-call | tf_op jit(solution)/shard_map/pallas_call | solution.py:706
  206.4 3.8 %shard_map.105 = (bf16[2048,128]{1,0:T(8,128)(2,1)}, bf16[3,2048,128]{2,1,0:T(8,128)(2,1)}) custom-call(bf16[2048,128]{1,0:T(8,128)(2,1)} %get-tuple-element.6.filter_in, bf16[3,2048,128]{2,1,0:T(8,128)(2,1)} %get-tuple-element.7.projected_in), custom_call_target="tpu_custom_call" | custom-call | tf_op jit(solution)/shard_map/pallas_call | solution.py:770

commit v6 on v5

--- a/solution.py
+++ b/solution.py
@@ -149,7 +149,7 @@
     def await_bytes(ref, sem):
         pltpu.make_async_copy(ref, ref, sem).wait()
 
-    early, middle = depth // 2, depth * 5 // 8
+    early, middle = 1, 2
     whole = chunks * slots
 
     def load_whole():
@@ -684,9 +684,27 @@
     await_bytes(whole_out.at[0, pl.ds(0, depth - 1)], send_sem.at[8, 0])
 
 
-def hand_over(filter_in, projected_in, filter_out, projected_out):
-    filter_out[...] = filter_in[...]
-    projected_out[...] = projected_in[...]
+def hand_over(filter_in, projected_in, filter_out, projected_out, passing, in_sem, out_sem):
+    half = filter_in.shape[0] // 2
+    copies = []
+    for k in range(8):
+        array, rows = k // 2, pl.ds(k % 2 * half, half)
+        source = projected_in.at[array, rows] if array < 3 else filter_in.at[rows]
+        target = projected_out.at[array, rows] if array < 3 else filter_out.at[rows]
+        held = passing.at[array, rows]
+        copies.append(
+            (
+                pltpu.make_async_copy(source, held, in_sem.at[k]),
+                pltpu.make_async_copy(held, target, out_sem.at[k]),
+            )
+        )
+    for first, _ in copies:
+        first.start()
+    for first, second in copies:
+        first.wait()
+        second.start()
+    for _, second in copies:
+        second.wait()
 
 
 def on_device(projected, short_taps, long_filter, skip_gain, cotangent):
@@ -762,20 +780,19 @@
         cotangent.reshape(channels, turns),
         *made,
     )
-    part = channels // 4
-    blocks = (
-        pl.BlockSpec((part, turns), lambda i: (i, 0)),
-        pl.BlockSpec((3, part, turns), lambda i: (0, i, 0)),
-    )
     filter_grad, projected_grad = pl.pallas_call(
         hand_over,
         out_shape=(
             jax.ShapeDtypeStruct((channels, turns), BF16),
             jax.ShapeDtypeStruct((3, channels, turns), BF16),
         ),
-        grid=(4,),
-        in_specs=blocks,
-        out_specs=blocks,
+        in_specs=[anywhere] * 2,
+        out_specs=(anywhere, anywhere),
+        scratch_shapes=[
+            vmem(4, channels, turns),
+            pltpu.SemaphoreType.DMA((8,)),
+            pltpu.SemaphoreType.DMA((8,)),
+        ],
         compiler_params=pltpu.CompilerParams(vmem_limit_bytes=56 << 20),
     )(filter_grad, projected_grad)
     return (

time: 211 us -> 206 us (0.976)
  Pallas kernels: 210 us -> 204 us
    pallas_call x1, Pallas kernels: 206 us -> 201 us  [on_device(): pl.pallas_call(functools.partial(kernel, planes, depth), out_shape=(jax.S...]
where the time goes in v6:
time: 206 us; the launch traced here: 204 us
  Pallas kernels  204 us (99%)
    pallas_call x1, Pallas kernels, on_device(): pl.pallas_call(functools.partial(kernel, planes, depth), out_shape=(jax.S...  201 us

profile of v6, /device:TPU:1, one launch (start us, length us, event | category | flops | bytes accessed | tf_op | source)
XLA Modules:
  0.0 204.2 jit_solution(15264866341909880727)
XLA Ops:
  0.6 201.2 %shard_map.104 = (bf16[2048,128]{1,0:T(8,128)(2,1)}, bf16[3,2048,128]{2,1,0:T(8,128)(2,1)}) custom-call(f32[3,3,2048]{2,1,0:T(4,128)} %bitcast.12, f32[1,2048]{1,0:T(1,128)} %bitcast.13, bf16[3,2048,128]{2,1,0:T(8,128)(2,1)} %bitcast.9, bf16[2048,128]{1,0:T(8,128)(2,1)} %bitcast.10, bf16[2048,128]{1,0:T(8,128)(2,1)} %bitcast.11, ...), custom_call_target="tpu_custom_call" | custom-call | tf_op jit(solution)/shard_map/pallas_call | solution.py:724
  201.8 2.4 %shard_map.105 = (bf16[2048,128]{1,0:T(8,128)(2,1)}, bf16[3,2048,128]{2,1,0:T(8,128)(2,1)}) custom-call(bf16[2048,128]{1,0:T(8,128)(2,1)} %get-tuple-element.6.filter_in, bf16[3,2048,128]{2,1,0:T(8,128)(2,1)} %get-tuple-element.7.projected_in), custom_call_target="tpu_custom_call" | custom-call | tf_op jit(solution)/shard_map/pallas_call | solution.py:783
